TPU v7x, 32 devices: a whole 2x2x4 slice. The times are simulated.
32 devices in a mesh: dp: 2 (over y), section: 4 (over x, core), head: 4 (over z).
Axes of the slice: x: 2, y: 2, z: 4, core: 2. Of those that a mesh axis runs over, the one named last changes fastest.
Arguments:
- images: bfloat16 [8, 144, 1408], P(('dp', 'head')), may hold values from -6 to 6
- w_in: bfloat16 [4, 1408, 3072], P('section'), may hold values from -0.15625 to 0.15625
- w_out: bfloat16 [4, 3072, 1408], P('section'), may hold values from -0.109375 to 0.109375
- fpn_weight: bfloat16 [2, 1408, 256], P(None, None, 'section'), may hold values from -0.15625 to 0.15625
- fc6_weight: bfloat16 [256, 49, 512], P('section'), may hold values from -0.0546875 to 0.0546875
- fc7_weight: bfloat16 [512, 512], replicated, may hold values from -0.25 to 0.25
- windows: int32 [3, 8, 128], P(None, ('dp', 'head')), may hold values from 0 to 8, as said below
- bilinear: float32 [2, 7, 4, 8, 128], P(None, None, None, ('dp', 'head')), may hold values from 0 to 1, as said below
- owners: int32 [8, 128, 1], P(('dp', 'head')), may hold values from 0 to 7; in each aligned block of 128 rows (0 to 127, 128 to 255, ..., all dimensions but the last counted through in order) at most 24 rows name the same one
- cotangent: bfloat16 [8, 8, 24, 512], P(('dp', 'head')), may hold values from -6 to 6
Outputs:
- grad_w_in: float32 [4, 1408, 3072], P('section', ('dp', 'head'))
- grad_w_out: float32 [4, 3072, 1408], P('section', ('dp', 'head'))
- grad_fpn: float32 [2, 1408, 256], P(None, None, 'section')
- grad_fc6: float32 [256, 49, 512], P('section', None, ('dp', 'head'))
- grad_fc7: float32 [512, 512], P(None, ('dp', 'head'))
Inputs may be any that keep to these rules, and one draw needn't show every extreme that they name: windows[0] is the level (0 or 1); windows[1] and windows[2] are a corner such that a 4x4 window fits the level's grid (12 or 6 cells a side). Along u each row of bilinear has at most two nonzero weights, on adjacent cells, summing to one. `owners`: among the 128 boxes of one image group (aligned blocks) no owner is named more than 24 times.
All inputs are finite; a program needn't handle non-finite values.
Results may differ from a plain program's by a relative error of at most 0.035.
Values may be sent and summed in bfloat16 or wider, within the bound.
A program may use at most 128 MiB of HBM per device.

v0:
```python
import math

import jax
import jax.numpy as jnp
from jax import lax
from jax.sharding import PartitionSpec as P

GRID = 12
SPAN = 4
POOLED = 7


EPS = 1e-06
GELU_C = math.sqrt(2.0 / math.pi)
HIGH = lax.Precision.HIGHEST


def passed_along(block, axis, distance):
    devices = range(lax.axis_size(axis))
    route = [(i - distance, i) for i in devices if i - distance in devices]
    return lax.ppermute(block, axis, route)


def broadcast(block, axis, holder):
    block = jnp.where(lax.axis_index(axis) == holder, block, jnp.zeros_like(block))
    return lax.psum(block, axis)


def gelu_parts(values):
    inner_arg = GELU_C * (values + 0.044715 * values * values * values)
    tangent = jnp.tanh(inner_arg)
    result = 0.5 * values * (1.0 + tangent)
    gelu_slope = 0.5 * (1.0 + tangent) + 0.5 * values * (1.0 - tangent * tangent) * GELU_C * (
        1.0 + 3.0 * 0.044715 * values * values
    )
    return (result, gelu_slope)


def norm_parts(tokens):
    floats = tokens.astype(jnp.float32)
    centred = floats - jnp.mean(floats, axis=-1, keepdims=True)
    scale_inv = lax.rsqrt(jnp.mean(centred * centred, axis=-1, keepdims=True) + EPS)
    return (centred * scale_inv, scale_inv)


def block_forward(tokens, w_first, w_second):
    normed, scale_inv = norm_parts(tokens)
    normed_b = normed.astype(jnp.bfloat16)
    preact = jnp.dot(normed_b, w_first, preferred_element_type=jnp.float32)
    activ, gelu_slope = gelu_parts(preact)
    activ_b = activ.astype(jnp.bfloat16)
    result = (
        tokens.astype(jnp.float32) + jnp.dot(activ_b, w_second, preferred_element_type=jnp.float32)
    ).astype(jnp.bfloat16)
    return (result, normed_b, preact, activ_b)


def block_backward(grad_out, tokens, preact, w_first, w_second):
    grad_act = jnp.dot(grad_out, w_second.T, preferred_element_type=jnp.float32)
    activ, gelu_slope = gelu_parts(preact)
    grad_pre = (grad_act * gelu_slope).astype(jnp.bfloat16)
    grad_norm = jnp.dot(grad_pre, w_first.T, preferred_element_type=jnp.float32)
    normed, scale_inv = norm_parts(tokens)
    grad_tok = scale_inv * (
        grad_norm
        - jnp.mean(grad_norm, axis=-1, keepdims=True)
        - normed * jnp.mean(grad_norm * normed, axis=-1, keepdims=True)
    )
    return ((grad_out.astype(jnp.float32) + grad_tok).astype(jnp.bfloat16), grad_pre)


def pyramid(top_rows, fpn_first, fpn_second, images_here):
    model_width = top_rows.shape[-1]
    half_grid = GRID // 2
    grid_rows = top_rows.reshape(images_here, GRID, GRID, model_width)
    pooled = (
        grid_rows.astype(jnp.float32)
        .reshape(images_here, half_grid, 2, half_grid, 2, model_width)
        .mean(axis=(2, 4))
        .astype(jnp.bfloat16)
    )
    level_one = jnp.dot(pooled, fpn_second, preferred_element_type=jnp.float32)
    upsampled = jnp.repeat(jnp.repeat(level_one, 2, axis=1), 2, axis=2)
    level_zero = jnp.dot(grid_rows, fpn_first, preferred_element_type=jnp.float32) + upsampled
    return (level_zero.astype(jnp.bfloat16), level_one.astype(jnp.bfloat16), pooled)


def pyramid_back(top_rows, pooled, fpn_first, fpn_second, grad_zero, grad_one):
    images_here = pooled.shape[0]
    half_grid = pooled.shape[1]
    channels = grad_zero.shape[-1]
    model_width = top_rows.shape[-1]
    grad_one = grad_one + grad_zero.reshape(images_here, half_grid, 2, half_grid, 2, channels).sum(
        axis=(2, 4)
    )
    zero_b = grad_zero.astype(jnp.bfloat16)
    one_b = grad_one.astype(jnp.bfloat16)
    grid_rows = top_rows.reshape(images_here, GRID, GRID, model_width)
    weight_zero = jnp.einsum("nyxd,nyxc->dc", grid_rows, zero_b, preferred_element_type=jnp.float32)
    weight_one = jnp.einsum("nyxd,nyxc->dc", pooled, one_b, preferred_element_type=jnp.float32)
    back_one = jnp.dot(one_b, fpn_second.T, preferred_element_type=jnp.float32)
    grad_top = jnp.dot(zero_b, fpn_first.T, preferred_element_type=jnp.float32) + 0.25 * jnp.repeat(
        jnp.repeat(back_one, 2, axis=1), 2, axis=2
    )
    return (weight_zero, weight_one, grad_top.reshape(images_here * GRID * GRID, model_width))


def window_rows(image_ids, anchor_y, anchor_x, side):
    offsets = jnp.arange(SPAN, dtype=jnp.int32)
    return (
        image_ids[:, None, None] * (side * side)
        + (anchor_y[:, None, None] + offsets[None, :, None]) * side
        + anchor_x[:, None, None]
        + offsets[None, None, :]
    )


def window_pair(image_ids, anchor_y, anchor_x):
    half_grid = GRID // 2
    near_y = jnp.minimum(anchor_y, half_grid - SPAN)
    near_x = jnp.minimum(anchor_x, half_grid - SPAN)
    return (
        window_rows(image_ids, anchor_y, anchor_x, GRID),
        window_rows(image_ids, near_y, near_x, half_grid),
    )


def make_crops(level_zero, level_one, image_ids, levels, anchor_y, anchor_x, weights_y, weights_x):
    channels = level_zero.shape[-1]
    rows_zero, rows_one = window_pair(image_ids, anchor_y, anchor_x)
    flat_zero = level_zero.reshape(-1, channels)
    flat_one = level_one.reshape(-1, channels)
    window_cells = jnp.where(
        (levels == 0)[:, None, None, None], flat_zero[rows_zero], flat_one[rows_one]
    ).astype(jnp.float32)
    crop_rows = jnp.einsum("kiu,kjv,kuvc->kcij", weights_y, weights_x, window_cells, precision=HIGH)
    return crop_rows.reshape(crop_rows.shape[0], -1).astype(jnp.bfloat16)


def spread_grads(
    grad_crops, image_ids, levels, anchor_y, anchor_x, weights_y, weights_x, images_here, channels
):
    half_grid = GRID // 2
    grad_cells = grad_crops.astype(jnp.float32).reshape(
        grad_crops.shape[0], channels, POOLED, POOLED
    )
    grad_window = jnp.einsum("kiu,kjv,kcij->kuvc", weights_y, weights_x, grad_cells, precision=HIGH)
    at_zero = (levels == 0)[:, None, None, None]
    rows_zero, rows_one = window_pair(image_ids, anchor_y, anchor_x)
    grad_zero = (
        jnp.zeros((images_here * GRID * GRID, channels), jnp.float32)
        .at[rows_zero.reshape(-1)]
        .add(jnp.where(at_zero, grad_window, 0.0).reshape(-1, channels))
    )
    grad_one = (
        jnp.zeros((images_here * half_grid * half_grid, channels), jnp.float32)
        .at[rows_one.reshape(-1)]
        .add(jnp.where(at_zero, 0.0, grad_window).reshape(-1, channels))
    )
    return (
        grad_zero.reshape(images_here, GRID, GRID, channels),
        grad_one.reshape(images_here, half_grid, half_grid, channels),
    )


def head_pass(slot_rows, fc6_flat, fc7_weight, cot_rows):
    partial_pre = jnp.dot(slot_rows, fc6_flat, preferred_element_type=jnp.float32)
    first_pre = lax.psum(partial_pre.astype(jnp.bfloat16), "section").astype(jnp.float32)
    first_act, first_slope = gelu_parts(first_pre)
    first_b = first_act.astype(jnp.bfloat16)
    second_pre = jnp.dot(first_b, fc7_weight, preferred_element_type=jnp.float32)
    second_act, second_slope = gelu_parts(second_pre)
    grad_second = (cot_rows * second_slope).astype(jnp.bfloat16)
    grad_fc7 = jnp.einsum("rh,rk->hk", first_b, grad_second, preferred_element_type=jnp.float32)
    grad_first = (
        jnp.dot(grad_second, fc7_weight.T, preferred_element_type=jnp.float32) * first_slope
    ).astype(jnp.bfloat16)
    grad_fc6 = jnp.einsum("rk,rh->kh", slot_rows, grad_first, preferred_element_type=jnp.float32)
    grad_slots = jnp.dot(grad_first, fc6_flat.T, preferred_element_type=jnp.float32).astype(
        jnp.bfloat16
    )
    return (grad_slots, grad_fc6, grad_fc7)


def slot_ranks(owner_ids, groups):
    onehot = (owner_ids[:, None] == jnp.arange(groups, dtype=jnp.int32)[None, :]).astype(jnp.int32)
    earlier = jnp.cumsum(onehot, axis=0) - onehot
    return jnp.sum(earlier * onehot, axis=1)


def keep_row(buffer, value, active, place_idx):
    return jnp.where(active, lax.dynamic_update_index_in_dim(buffer, value, place_idx, 0), buffer)


def per_device(
    images, w_in, w_out, fpn_weight, fc6_weight, fc7_weight, windows, bilinear, owners, cotangent
):
    sections = lax.axis_size("section")
    section_idx = lax.axis_index("section")
    groups = lax.axis_size(("dp", "head"))
    images_here = images.shape[0]
    tokens_img = images.shape[1]
    model_width = images.shape[2]
    w_first = w_in[0]
    w_second = w_out[0]
    inner_width = w_first.shape[1]
    last_section = sections - 1
    tick_count = images_here + sections - 1

    def forward_tick(step, state_in):
        incoming, kept_x, kept_normed, kept_pre, kept_act, kept_top = state_in
        micro_idx = step - section_idx
        active = (micro_idx >= 0) & (micro_idx < images_here)
        place_idx = jnp.clip(micro_idx, 0, images_here - 1)
        fresh_rows = lax.dynamic_index_in_dim(images, place_idx, 0, keepdims=False)
        tokens = jnp.where(section_idx == 0, fresh_rows, incoming)
        result, normed_b, preact, activ_b = block_forward(tokens, w_first, w_second)
        result = jnp.where(active, result, jnp.zeros_like(result))
        kept_top = jnp.where(
            section_idx == last_section, keep_row(kept_top, result, active, place_idx), kept_top
        )
        incoming = passed_along(result, "section", 1)
        return (
            incoming,
            keep_row(kept_x, tokens, active, place_idx),
            keep_row(kept_normed, normed_b, active, place_idx),
            keep_row(kept_pre, preact, active, place_idx),
            keep_row(kept_act, activ_b, active, place_idx),
            kept_top,
        )

    token_zeros = jnp.zeros((images_here, tokens_img, model_width), jnp.bfloat16)
    start_state = (
        jnp.zeros((tokens_img, model_width), jnp.bfloat16),
        token_zeros,
        token_zeros,
        jnp.zeros((images_here, tokens_img, inner_width), jnp.float32),
        jnp.zeros((images_here, tokens_img, inner_width), jnp.bfloat16),
        token_zeros,
    )
    incoming, kept_x, kept_normed, kept_pre, kept_act, kept_top = lax.fori_loop(
        0, tick_count, forward_tick, start_state
    )
    top_all = broadcast(kept_top, "section", last_section)
    top_rows = top_all.reshape(images_here * tokens_img, model_width)
    level_zero, level_one, pooled = pyramid(top_rows, fpn_weight[0], fpn_weight[1], images_here)
    channels = level_zero.shape[-1]
    box_count = windows.shape[2]
    per_group = images_here * box_count
    levels = windows[0].reshape(per_group)
    anchor_y = windows[1].reshape(per_group)
    anchor_x = windows[2].reshape(per_group)
    weights_y = jnp.transpose(bilinear[0].reshape(POOLED, SPAN, per_group), (2, 0, 1))
    weights_x = jnp.transpose(bilinear[1].reshape(POOLED, SPAN, per_group), (2, 0, 1))
    owner_ids = owners.reshape(per_group)
    image_ids = jnp.repeat(jnp.arange(images_here, dtype=jnp.int32), box_count)
    slot_rank = slot_ranks(owner_ids, groups)
    capacity = cotangent.shape[2]
    head_units = cotangent.shape[3]
    cot_rows = cotangent[0].reshape(groups * capacity, head_units).astype(jnp.float32)
    fc6_flat = fc6_weight.reshape(-1, head_units)
    crop_rows = make_crops(
        level_zero, level_one, image_ids, levels, anchor_y, anchor_x, weights_y, weights_x
    )
    outgoing = (
        jnp.zeros((groups, capacity, crop_rows.shape[1]), jnp.bfloat16)
        .at[owner_ids, slot_rank]
        .set(crop_rows)
    )
    arrived = lax.all_to_all(outgoing, ("dp", "head"), split_axis=0, concat_axis=0, tiled=True)
    slot_rows = arrived.reshape(groups * capacity, -1)
    grad_slots, grad_fc6, grad_fc7 = head_pass(slot_rows, fc6_flat, fc7_weight, cot_rows)
    returned = lax.all_to_all(
        grad_slots.reshape(groups, capacity, -1),
        ("dp", "head"),
        split_axis=0,
        concat_axis=0,
        tiled=True,
    )
    grad_crops = returned[owner_ids, slot_rank]
    grad_zero, grad_one = spread_grads(
        grad_crops,
        image_ids,
        levels,
        anchor_y,
        anchor_x,
        weights_y,
        weights_x,
        images_here,
        channels,
    )
    fc6_part, fc7_part = (
        lax.psum_scatter(
            grad_fc6.reshape(channels, POOLED * POOLED, head_units).astype(jnp.bfloat16),
            ("dp", "head"),
            scatter_dimension=2,
            tiled=True,
        ).astype(jnp.float32),
        lax.psum_scatter(
            grad_fc7.astype(jnp.bfloat16), ("dp", "head"), scatter_dimension=1, tiled=True
        ).astype(jnp.float32),
    )
    weight_zero, weight_one, grad_part = pyramid_back(
        top_rows, pooled, fpn_weight[0], fpn_weight[1], grad_zero, grad_one
    )
    fpn_zero, fpn_one = (
        lax.psum(weight_zero.astype(jnp.bfloat16), ("dp", "head")).astype(jnp.float32),
        lax.psum(weight_one.astype(jnp.bfloat16), ("dp", "head")).astype(jnp.float32),
    )
    grad_total = lax.psum(grad_part.astype(jnp.bfloat16), "section")
    grad_top = grad_total.reshape(images_here, tokens_img, model_width)

    def backward_tick(step, state_in):
        incoming, kept_grad_pre, kept_grad_out = state_in
        micro_idx = step - (last_section - section_idx)
        active = (micro_idx >= 0) & (micro_idx < images_here)
        place_idx = jnp.clip(micro_idx, 0, images_here - 1)
        top_grad = lax.dynamic_index_in_dim(grad_top, place_idx, 0, keepdims=False)
        grad_out = jnp.where(section_idx == last_section, top_grad, incoming)
        layer_in = lax.dynamic_index_in_dim(kept_x, place_idx, 0, keepdims=False)
        layer_pre = lax.dynamic_index_in_dim(kept_pre, place_idx, 0, keepdims=False)
        grad_in, grad_pre = block_backward(grad_out, layer_in, layer_pre, w_first, w_second)
        grad_in = jnp.where(active, grad_in, jnp.zeros_like(grad_in))
        incoming = passed_along(grad_in, "section", -1)
        return (
            incoming,
            keep_row(kept_grad_pre, grad_pre, active, place_idx),
            keep_row(kept_grad_out, grad_out, active, place_idx),
        )

    back_state = (
        jnp.zeros((tokens_img, model_width), jnp.bfloat16),
        jnp.zeros((images_here, tokens_img, inner_width), jnp.bfloat16),
        token_zeros,
    )
    incoming, kept_grad_pre, kept_grad_out = lax.fori_loop(0, tick_count, backward_tick, back_state)
    normed_flat = kept_normed.reshape(-1, model_width)
    act_flat = kept_act.reshape(-1, inner_width)
    grad_pre_flat = kept_grad_pre.reshape(-1, inner_width)
    grad_out_flat = kept_grad_out.reshape(-1, model_width)
    columns = normed_flat
    grad_first = lax.psum_scatter(
        jnp.einsum("rd,rf->df", columns, grad_pre_flat, preferred_element_type=jnp.float32).astype(
            jnp.bfloat16
        ),
        ("dp", "head"),
        scatter_dimension=0,
        tiled=True,
    ).astype(jnp.float32)
    columns = act_flat
    grad_second = lax.psum_scatter(
        jnp.einsum("rf,rd->fd", columns, grad_out_flat, preferred_element_type=jnp.float32).astype(
            jnp.bfloat16
        ),
        ("dp", "head"),
        scatter_dimension=0,
        tiled=True,
    ).astype(jnp.float32)
    return (grad_first[None], grad_second[None], jnp.stack([fpn_zero, fpn_one]), fc6_part, fc7_part)


def solution(mesh):
    return jax.shard_map(
        per_device,
        mesh=mesh,
        in_specs=(
            P(("dp", "head"), None, None),
            P("section", None, None),
            P("section", None, None),
            P(None, None, "section"),
            P("section", None, None),
            P(),
            P(None, ("dp", "head"), None),
            P(None, None, None, ("dp", "head"), None),
            P(("dp", "head"), None, None),
            P(("dp", "head"), None, None, None),
        ),
        out_specs=(
            P("section", ("dp", "head"), None),
            P("section", ("dp", "head"), None),
            P(None, None, "section"),
            P("section", None, ("dp", "head")),
            P(None, ("dp", "head")),
        ),
        check_vma=False,
    )
```

profile of v0, /device:TPU:0, one launch (start us, length us, event | category | flops | bytes accessed | tf_op | source)
XLA Modules:
  0.0 908.5 jit_solution(11442635793176559128)
XLA Ops:
  8.1 79.4 %while.45 = (s32[]{:T(128)}, bf16[144,1408]{1,0:T(8,128)(2,1)}, bf16[1,144,1408]{2,1,0:T(8,128)(2,1)S(1)}, bf16[1,144,1408]{2,1,0:T(8,128)(2,1)S(1)}, f32[1,144,...) while((s32[]{:T(128)}, bf16[144,1408]{1,0:T(8,128)(2,1)}, ...), condition=%wide.region_3.4_spmd.clone, body=%wide.region_0.3_spmd.clone.sunk | while | flops 2506420224 | bytes 78981736 | solution.py:241
  35.3 7.7 collective-permute-start
  91.2 35.5 %all-reduce.6.cloned.1.call-done = bf16[1,144,1408]{2,1,0:T(8,128)(2,1)} async-done(((bf16[1,144,1408]{2,1,0:T(8,128)(2,1)}), bf16[1,144,1408]{2,1,0:T(8,128)(2,1)}) %all-reduce.6.cloned.1.call-update) | async-done | bytes 405520 | tf_op jit(solution)/shard_map/psum | solution.py:26
  137.9 8.1 gather_fusion
  160.7 28.5 %scatter_fusion = bf16[8,24,3136]{2,1,0:T(8,128)(2,1)} fusion(bf16[8,24,3136]{2,1,0:T(8,128)(2,1)} %broadcast_in_dim.173, s32[128]{0:T(128)S(1)} %get-tuple-element.625, bf16[128,3136]{1,0:T(8,128)(2,1)S(1)} %copy.47), kind=kCustom, calls=%fused_computation.3 | custom fusion | bytes 2409472 | tf_op jit(solution)/shard_map/scatter | solution.py:268
  204.4 19.5 %all-to-all-done = bf16[8,24,3136]{2,1,0:T(8,128)(2,1)S(1)} async-done(((bf16[8,24,3136]{2,1,0:T(8,128)(2,1)}), bf16[8,24,3136]{2,1,0:T(8,128)(2,1)S(1)}, u32[]{:S(2)}, u32[]{:S(2)}) %all-to-all-start) | async-done | bytes 1204256 | tf_op jit(solution)/shard_map/all_to_all | solution.py:270
  227.8 28.8 %all-reduce.8.cloned.1.call-done = bf16[192,512]{1,0:T(8,128)(2,1)} async-done(((bf16[192,512]{1,0:T(8,128)(2,1)}), bf16[192,512]{1,0:T(8,128)(2,1)}) %all-reduce.8.cloned.1.call-update) | async-done | bytes 196624 | tf_op jit(solution)/shard_map/psum | solution.py:168
  267.9 28.2 %all-to-all-done.1 = bf16[8,24,3136]{2,1,0:T(8,128)(2,1)S(1)} async-done(((bf16[8,24,3136]{2,1,0:T(8,128)(2,1)}), bf16[8,24,3136]{2,1,0:T(8,128)(2,1)S(1)}, u32[]{:S(2)}, u32[]{:S(2)}) %all-to-all-start.1) | async-done | bytes 1204256 | tf_op jit(solution)/shard_map/all_to_all | solution.py:273
  309.2 12.0 %scatter_custom_fusion.1 = f32[144,64]{1,0:T(8,128)S(1)} fusion(s32[2048]{0:T(1024)S(1)} %bitcast.264, f32[2048,64]{1,0:T(8,128)} %bitcast.258, f32[]{:T(128)} %constant.276.clone.1), kind=kCustom, calls=%fused_computation.153 | custom fusion | flops 131072 | bytes 37376 | tf_op jit(solution)/shard_map/scatter-add | solution.py:153
  321.4 11.5 %scatter_custom_fusion.2 = f32[36,64]{1,0:T(8,128)S(1)} fusion(s32[2048]{0:T(1024)S(1)} %bitcast.263, f32[2048,64]{1,0:T(8,128)S(1)} %bitcast.257, f32[]{:T(128)} %constant.276.clone.1), kind=kCustom, calls=%fused_computation.157 | custom fusion | flops 131072 | bytes 9220 | tf_op jit(solution)/shard_map/scatter-add | solution.py:158
  341.5 10.0 %reshape.525 = bf16[64,49,192]{1,0,2:T(8,128)(2,1)} reshape(bf16[3136,192]{0,1:T(8,128)(2,1)S(1)} %bitcast.253) | data formatting | bytes 2408448 | tf_op jit(solution)/shard_map/rk,rh->kh/dot_general | solution.py:178
  360.2 8.9 copy.58
  369.2 9.6 %reshape.526 = bf16[512,3136]{1,0:T(8,128)(2,1)} reshape(bf16[512,49,64]{2,1,0:T(8,128)(2,1)} %bitcast.250) | data formatting | bytes 6422528
  380.4 87.6 %while.46 = (s32[]{:T(128)}, bf16[144,1408]{1,0:T(8,128)(2,1)}, bf16[1,144,3072]{2,1,0:T(8,128)(2,1)}, bf16[1,144,1408]{2,1,0:T(8,128)(2,1)S(1)}, s32[]{:T(128)}...) while((s32[]{:T(128)}, bf16[144,1408]{1,0:T(8,128)(2,1)}, ...), condition=%wide.region_19.20_spmd.clone, body=%wide.region_14.19_spmd.clone.sunk | while | flops 2505978112 | bytes 65383472 | solution.py:336
  382.3 7.1 bitcast_select_fusion.21
  400.3 7.1 bitcast_select_fusion.21
  422.8 7.1 bitcast_select_fusion.21
  435.6 8.1 collective-permute-done.1
  446.4 7.2 bitcast_select_fusion.21
  459.2 8.1 collective-permute-done.1
  482.7 23.7 %all-reduce.12.cloned.1.call-done = (bf16[1,1408,64]{1,2,0:T(8,128)(2,1)}, bf16[1,1408,64]{1,2,0:T(8,128)(2,1)}) async-done(((bf16[1,1408,64]{1,2,0:T(8,128)(2,1)}, bf16[1,1408,64]{1,2,0:T(8,128)(2,1)}), (bf16[1,1408,64]{1,2,0:T(8,128)(2,1)}, bf16[1,1408,64]{1,2,0:T(8,128)(2,1)})) %all-reduce.12.cloned.1.call-update) | async-done | bytes 360464 | tf_op jit(solution)/shard_map/psum | solution.py:308
  508.3 77.5 %reduce-scatter.13.cloned.1.call-done = bf16[64,3136]{1,0:T(8,128)(2,1)} async-done(((bf16[512,3136]{1,0:T(8,128)(2,1)}), bf16[64,3136]{1,0:T(8,128)(2,1)}) %reduce-scatter.13.cloned.1.call-update) | async-done | bytes 401424
  590.3 151.7 %reduce-scatter.7.cloned.1.call-done = bf16[176,3072]{1,0:T(8,128)(2,1)} async-done(((bf16[1408,3072]{1,0:T(8,128)(2,1)}), bf16[176,3072]{1,0:T(8,128)(2,1)}) %reduce-scatter.7.cloned.1.call-update) | async-done | bytes 1081360 | tf_op jit(solution)/shard_map/reduce_scatter | solution.py:342
  744.8 153.7 %reduce-scatter.9.cloned.1.call-done = bf16[384,1408]{1,0:T(8,128)(2,1)} async-done(((bf16[3072,1408]{1,0:T(8,128)(2,1)}), bf16[384,1408]{1,0:T(8,128)(2,1)}) %reduce-scatter.9.cloned.1.call-update) | async-done | bytes 1081360 | tf_op jit(solution)/shard_map/reduce_scatter | solution.py:351
  (361 shorter events, 232.4 us)
Async XLA Ops:
  7.2 249.5 %copy-start = (bf16[512,512]{1,0:T(8,128)(2,1)S(1)}, bf16[512,512]{1,0:T(8,128)(2,1)}, u32[]{:S(2)}) copy-start(bf16[512,512]{1,0:T(8,128)(2,1)} %param.19) | copy-start | bytes 1572868
  7.2 119.5 %all-reduce.6.cloned.1.call-start = ((), (), s32[]{:S(2)}) async-start(), calls=%async_computation.6 | async-start | bytes 811008 | tf_op jit(solution)/shard_map/psum | solution.py:26
  8.1 80.2 %copy-start.32 = (s32[3,1,128]{2,1,0:T(1,128)S(1)}, s32[3,1,128]{2,1,0:T(1,128)}, u32[]{:S(2)}) copy-start(s32[3,1,128]{2,1,0:T(1,128)} %param.20) | copy-start | bytes 4612
  8.1 80.2 %copy-start.30 = (f32[2,7,4,1,128]{4,3,2,1,0:T(1,128)S(1)}, f32[2,7,4,1,128]{4,3,2,1,0:T(1,128)}, u32[]{:S(2)}) copy-start(f32[2,7,4,1,128]{4,3,2,1,0:T(1,128)} %param.21) | copy-start | bytes 86020
  8.1 80.4 %copy-start.31 = (s32[1,128,1]{1,2,0:T(1,128)S(1)}, s32[1,128,1]{1,2,0:T(1,128)}, u32[]{:S(2)}) copy-start(s32[1,128,1]{1,2,0:T(1,128)} %param.22) | copy-start | bytes 1540
  19.1 5.2 collective-permute-start
  35.3 10.9 %collective-permute-start = (bf16[144,1408]{1,0:T(8,128)(2,1)}, bf16[144,1408]{1,0:T(8,128)(2,1)}, u32[]{:S(2)}, u32[]{:S(2)}) collective-permute-start(bf16[144,1408]{1,0:T(8,128)(2,1)} %get-tuple-element.798), channel_id=1, source_target_pairs={{0,4},{4,8},{8,12},{1,5},{5,9},{9,13},{2,6},{6,10},{10,14},{3,7},{... | collective-permute-start | bytes 1216520 | tf_op jit(solution)/shard_map/while/body/eval_jaxpr/ppermute | solution.py:21
  57.2 9.6 %collective-permute-start = (bf16[144,1408]{1,0:T(8,128)(2,1)}, bf16[144,1408]{1,0:T(8,128)(2,1)}, u32[]{:S(2)}, u32[]{:S(2)}) collective-permute-start(bf16[144,1408]{1,0:T(8,128)(2,1)} %get-tuple-element.798), channel_id=1, source_target_pairs={{0,4},{4,8},{8,12},{1,5},{5,9},{9,13},{2,6},{6,10},{10,14},{3,7},{... | collective-permute-start | bytes 1216520 | tf_op jit(solution)/shard_map/while/body/eval_jaxpr/ppermute | solution.py:21
  77.8 9.6 %collective-permute-start = (bf16[144,1408]{1,0:T(8,128)(2,1)}, bf16[144,1408]{1,0:T(8,128)(2,1)}, u32[]{:S(2)}, u32[]{:S(2)}) collective-permute-start(bf16[144,1408]{1,0:T(8,128)(2,1)} %get-tuple-element.798), channel_id=1, source_target_pairs={{0,4},{4,8},{8,12},{1,5},{5,9},{9,13},{2,6},{6,10},{10,14},{3,7},{... | collective-permute-start | bytes 1216520 | tf_op jit(solution)/shard_map/while/body/eval_jaxpr/ppermute | solution.py:21
  88.5 59.7 %copy-start.14 = (f32[1,7,4,1,128]{1,2,4,3,0:T(4,128)}, f32[1,7,4,1,128]{1,2,4,3,0:T(4,128)S(1)}, u32[]{:S(2)}) copy-start(f32[1,7,4,1,128]{1,2,4,3,0:T(4,128)S(1)} %copy.61) | copy-start | bytes 43012
  189.2 34.7 %all-to-all-start = ((bf16[8,24,3136]{2,1,0:T(8,128)(2,1)}), bf16[8,24,3136]{2,1,0:T(8,128)(2,1)S(1)}, u32[]{:S(2)}, u32[]{:S(2)}) async-start(bf16[8,24,3136]{2,1,0:T(8,128)(2,1)} %scatter_fusion), calls=%async_computation | async-start | bytes 2457600 | tf_op jit(solution)/shard_map/all_to_all | solution.py:270
  194.1 62.5 %all-reduce.8.cloned.1.call-start = ((), (), s32[]{:S(2)}) async-start(), calls=%async_computation.7 | async-start | bytes 393216 | tf_op jit(solution)/shard_map/psum | solution.py:168
  261.0 35.1 %all-to-all-start.1 = ((bf16[8,24,3136]{2,1,0:T(8,128)(2,1)}), bf16[8,24,3136]{2,1,0:T(8,128)(2,1)S(1)}, u32[]{:S(2)}, u32[]{:S(2)}) async-start(bf16[8,24,3136]{2,1,0:T(8,128)(2,1)} %bitcast.254), calls=%async_computation.1 | async-start | bytes 2457600 | tf_op jit(solution)/shard_map/all_to_all | solution.py:273
  266.7 112.4 %all-reduce.10.cloned.1.call-start = ((), (), s32[]{:S(2)}) async-start(), calls=%async_computation.8 | async-start | bytes 811008 | tf_op jit(solution)/shard_map/psum | solution.py:310
  337.1 144.1 %reduce-scatter.11.cloned.1.call-start = ((), (), s32[]{:S(2)}) async-start(), calls=%async_computation.11 | async-start | bytes 589824 | tf_op jit(solution)/shard_map/reduce_scatter | solution.py:299
  339.5 166.9 %all-reduce.12.cloned.1.call-start = ((), (), s32[]{:S(2)}) async-start(), calls=%async_computation.13 | async-start | bytes 720896 | tf_op jit(solution)/shard_map/psum | solution.py:308
  341.5 244.3 %reduce-scatter.13.cloned.1.call-start = ((), (), s32[]{:S(2)}) async-start(), calls=%async_computation.12 | async-start | bytes 3686400
  378.8 363.1 %reduce-scatter.7.cloned.1.call-start = ((), (), s32[]{:S(2)}) async-start(), calls=%async_computation.9 | async-start | bytes 9732096 | tf_op jit(solution)/shard_map/reduce_scatter | solution.py:342
  393.8 3.8 collective-permute-start.1
  411.8 8.3 collective-permute-start.1
  434.3 9.4 %collective-permute-start.1 = (bf16[144,1408]{1,0:T(8,128)(2,1)}, bf16[144,1408]{1,0:T(8,128)(2,1)S(1)}, u32[]{:S(2)}, u32[]{:S(2)}) collective-permute-start(bf16[144,1408]{1,0:T(8,128)(2,1)} %fusion.144), channel_id=1, source_target_pairs={{4,0},{8,4},{12,8},{5,1},{9,5},{13,9},{6,2},{10,6},{14,10},{7,3},{... | collective-permute-start | bytes 1216520 | tf_op jit(solution)/shard_map/while/body/eval_jaxpr/ppermute | solution.py:21
  457.9 9.4 %collective-permute-start.1 = (bf16[144,1408]{1,0:T(8,128)(2,1)}, bf16[144,1408]{1,0:T(8,128)(2,1)S(1)}, u32[]{:S(2)}, u32[]{:S(2)}) collective-permute-start(bf16[144,1408]{1,0:T(8,128)(2,1)} %fusion.144), channel_id=1, source_target_pairs={{4,0},{8,4},{12,8},{5,1},{9,5},{13,9},{6,2},{10,6},{14,10},{7,3},{... | collective-permute-start | bytes 1216520 | tf_op jit(solution)/shard_map/while/body/eval_jaxpr/ppermute | solution.py:21
  475.0 423.5 %reduce-scatter.9.cloned.1.call-start = ((), (), s32[]{:S(2)}) async-start(), calls=%async_computation.10 | async-start | bytes 9732096 | tf_op jit(solution)/shard_map/reduce_scatter | solution.py:351
  741.9 159.3 %copy-start.1 = (bf16[512,512]{1,0:T(8,128)(2,1)S(1)}, bf16[512,512]{1,0:T(8,128)(2,1)}, u32[]{:S(2)}) copy-start(bf16[512,512]{1,0:T(8,128)(2,1)} %param.19) | copy-start | bytes 1572868
  (75 other events, 371.4 us)
Sparse Core Ops, SparseCore 0:
  88.4 38.2 all-reduce.5
  227.9 28.6 all-reduce.7
  337.2 29.1 all-reduce.9
  370.5 62.2 reduce-scatter.10
  436.1 70.2 all-reduce.11
  510.3 75.4 reduce-scatter.12
  589.4 152.4 reduce-scatter.6
  746.0 152.5 reduce-scatter.8
where the time goes:
time: 919 us; the launch traced here: 909 us
  waiting for transfers between devices  545 us (59%)
  local copies, waits for them, and re-layouts  123 us (13%)
  matrix products  118 us (13%)
  other arithmetic  67 us (7%)
  starting transfers between devices  40.2 us (4%)
  between operations  15.3 us (2%)
    reduce_scatter x1, waiting for transfers between devices, per_device(): lax.psum_scatter(jnp.einsum('rf,rd->fd', columns, grad_out_flat, preferre...  154 us
    reduce_scatter x1, waiting for transfers between devices, per_device(): lax.psum_scatter(jnp.einsum('rd,rf->df', columns, grad_pre_flat, preferre...  152 us
    unnamed x9, waiting for transfers between devices  77.6 us
    psum x1, waiting for transfers between devices, broadcast(): return lax.psum(block, axis)  35.5 us
    unnamed x65, local copies, waits for them, and re-layouts  30.1 us
    ppermute x8, starting transfers between devices, passed_along(): return lax.ppermute(block, axis, route)  28.9 us
    psum x1, waiting for transfers between devices, head_pass(): lax.psum(partial_pre.astype(jnp.bfloat16), 'section').astype(jnp.float32)  28.8 us
    dot_general x4, matrix products, block_backward(): grad_act = jnp.dot(grad_out, w_second.T, preferred_element_type=jnp.float32)  28.6 us
  transfers between devices with their start and end apart: 18, of which 12 were waited for; matrix products, arithmetic and copies ran while one was open for 16% of the time, Pallas kernels for 0%

commit v1 on v0

v1 whole, which is shorter than its diff:
```python
import math

import jax
import jax.numpy as jnp
from jax import lax
from jax.sharding import PartitionSpec as P

GRID = 12
SPAN = 4
POOLED = 7


EPS = 1e-06
GELU_C = math.sqrt(2.0 / math.pi)
HIGH = lax.Precision.HIGHEST


def moved(block, axis, route):
    return lax.ppermute(block, axis, route)


def spread_from_last(block, axis):
    size = lax.axis_size(axis)
    place = lax.axis_index(axis)
    last = size - 1
    stride = size // 2
    while stride >= 1:
        route = [(i, i - stride) for i in range(size) if (last - i) % (2 * stride) == 0]
        arrived = moved(block, axis, route)
        takes = (last - place) % (2 * stride) == stride
        block = jnp.where(takes, arrived, block)
        stride //= 2
    return block


def sum_to_last(block, axis):
    size = lax.axis_size(axis)
    last = size - 1
    total = block.astype(jnp.float32)
    stride = 1
    while stride < size:
        route = [(i - stride, i) for i in range(size) if (last - i) % (2 * stride) == 0]
        arrived = moved(total.astype(jnp.bfloat16), axis, route)
        total = total + arrived.astype(jnp.float32)
        stride *= 2
    return total.astype(jnp.bfloat16)


def sum_everywhere(block, axis):
    size = lax.axis_size(axis)
    terms = [block] + [
        moved(block, axis, [(i, i ^ distance) for i in range(size)]) for distance in range(1, size)
    ]
    terms = [term.astype(jnp.float32) for term in terms]
    while len(terms) > 1:
        terms = [terms[i] + terms[i + 1] for i in range(0, len(terms), 2)]
    return terms[0]


def gelu_parts(values):
    inner_arg = GELU_C * (values + 0.044715 * values * values * values)
    tangent = jnp.tanh(inner_arg)
    result = 0.5 * values * (1.0 + tangent)
    gelu_slope = 0.5 * (1.0 + tangent) + 0.5 * values * (1.0 - tangent * tangent) * GELU_C * (
        1.0 + 3.0 * 0.044715 * values * values
    )
    return (result, gelu_slope)


def norm_parts(tokens):
    floats = tokens.astype(jnp.float32)
    centred = floats - jnp.mean(floats, axis=-1, keepdims=True)
    scale_inv = lax.rsqrt(jnp.mean(centred * centred, axis=-1, keepdims=True) + EPS)
    return (centred * scale_inv, scale_inv)


def dot(left, right):
    return jnp.dot(left, right, preferred_element_type=jnp.float32)


def dot_nt(left, right):
    return jnp.einsum("rk,ck->rc", left, right, preferred_element_type=jnp.float32)


def dot_tn(left, right):
    return jnp.einsum("kr,kc->rc", left, right, preferred_element_type=jnp.float32)


def block_forward(tokens, w_first, w_second):
    normed, scale_inv = norm_parts(tokens)
    activ, gelu_slope = gelu_parts(dot(normed.astype(jnp.bfloat16), w_first))
    return (tokens.astype(jnp.float32) + dot(activ.astype(jnp.bfloat16), w_second)).astype(
        jnp.bfloat16
    )


def block_backward(grad_out, normed, scale_inv, slope, w_first, w_second):
    grad_pre = (dot_nt(grad_out, w_second) * slope).astype(jnp.bfloat16)
    grad_norm = dot_nt(grad_pre, w_first)
    grad_tok = scale_inv * (
        grad_norm
        - jnp.mean(grad_norm, axis=-1, keepdims=True)
        - normed * jnp.mean(grad_norm * normed, axis=-1, keepdims=True)
    )
    return (grad_out.astype(jnp.float32) + grad_tok).astype(jnp.bfloat16)


def parents():
    half = GRID // 2
    cells = jnp.arange(GRID * GRID, dtype=jnp.int32)
    parent = (cells // GRID // 2) * half + (cells % GRID) // 2
    return (parent[:, None] == jnp.arange(half * half, dtype=jnp.int32)[None, :])


def sampling_rows(windows, bilinear):
    half = GRID // 2
    levels, anchor_y, anchor_x = (windows[i][:, None] for i in range(3))
    fine = jnp.arange(GRID * GRID, dtype=jnp.int32)
    coarse = jnp.arange(half * half, dtype=jnp.int32)
    cell_level = jnp.concatenate([jnp.zeros_like(fine), jnp.ones_like(coarse)])[None]
    cell_y = jnp.concatenate([fine // GRID, coarse // half])[None]
    cell_x = jnp.concatenate([fine % GRID, coarse % half])[None]
    offset_y = jnp.where(levels == cell_level, cell_y - anchor_y, -1)
    offset_x = cell_x - anchor_x
    rows = sum(
        bilinear[0][:, u, :, None] * (offset_y == u).astype(jnp.float32)[None] for u in range(SPAN)
    )
    cols = sum(
        bilinear[1][:, v, :, None] * (offset_x == v).astype(jnp.float32)[None] for v in range(SPAN)
    )
    weights = (rows[:, None] * cols[None]).astype(jnp.bfloat16)
    return weights.reshape(-1, weights.shape[-1])


def box_cotangents(cotangent, owner_ids):
    groups, capacity, units = cotangent.shape
    arrived = lax.all_to_all(cotangent, ("dp", "head"), split_axis=0, concat_axis=0, tiled=True)
    count = owner_ids.shape[0]
    order = jnp.arange(count, dtype=jnp.int32)
    earlier = (owner_ids[:, None] == owner_ids[None, :]) & (order[None, :] < order[:, None])
    rank = jnp.sum(earlier.astype(jnp.int32), axis=1)
    slot = owner_ids * capacity + rank
    pick = slot[:, None] == jnp.arange(groups * capacity, dtype=jnp.int32)[None, :]
    return dot(pick.astype(jnp.bfloat16), arrived.reshape(groups * capacity, units))


def per_device(
    images, w_in, w_out, fpn_weight, fc6_weight, fc7_weight, windows, bilinear, owners, cotangent
):
    axes = ("dp", "head")
    sections = lax.axis_size("section")
    section_idx = lax.axis_index("section")
    groups = lax.axis_size(axes)
    group_idx = lax.axis_index(axes)
    last_section = sections - 1
    w_first = w_in[0]
    w_second = w_out[0]
    model_width, inner_width = w_first.shape
    channels = fpn_weight.shape[2]
    head_units = fc7_weight.shape[0]
    boxes = windows.shape[2]
    taps = POOLED * POOLED
    fine_cells = GRID * GRID

    cot_rows = box_cotangents(cotangent[0], owners.reshape(boxes))
    weights = sampling_rows(windows[:, 0], bilinear[:, :, :, 0])
    fc6_taps = jnp.transpose(fc6_weight, (1, 0, 2)).reshape(taps * channels, head_units)

    tokens = images[0]
    kept_tokens = tokens
    for step in range(sections):
        if step:
            route = [(i, i + 1) for i in range(sections - 1)]
            tokens = moved(result, "section", route)
            kept_tokens = jnp.where(section_idx == step, tokens, kept_tokens)
        result = block_forward(tokens, w_first, w_second)
    top = spread_from_last(result, "section")

    all_tokens = lax.all_gather(kept_tokens, axes, axis=0, tiled=True)

    up = parents()
    up_b = up.astype(jnp.bfloat16)
    up_f = up.astype(jnp.float32)
    pooled = (0.25 * dot_tn(up_b, top)).astype(jnp.bfloat16)
    level_one = dot(pooled, fpn_weight[1])
    level_zero = dot(top, fpn_weight[0]) + jnp.dot(up_f, level_one, precision=HIGH)
    cells = jnp.concatenate([level_zero, level_one], axis=0).astype(jnp.bfloat16)
    crops = dot(weights, cells).astype(jnp.bfloat16).reshape(taps, boxes, channels)
    crop_rows = jnp.transpose(crops, (1, 0, 2)).reshape(boxes, taps * channels)
    first_pre = sum_everywhere(dot(crop_rows, fc6_taps).astype(jnp.bfloat16), "section")

    normed_own, scale_own = norm_parts(kept_tokens)
    slope_own = gelu_parts(dot(normed_own.astype(jnp.bfloat16), w_first))[1]

    first_act, first_slope = gelu_parts(first_pre)
    first_b = first_act.astype(jnp.bfloat16)
    second_slope = gelu_parts(dot(first_b, fc7_weight))[1]
    grad_second = (cot_rows * second_slope).astype(jnp.bfloat16)
    grad_first = (dot_nt(grad_second, fc7_weight) * first_slope).astype(jnp.bfloat16)
    grad_crops = dot_nt(grad_first, fc6_taps).astype(jnp.bfloat16)
    grad_crops = jnp.transpose(grad_crops.reshape(boxes, taps, channels), (1, 0, 2))
    grad_cells = dot_tn(weights, grad_crops.reshape(taps * boxes, channels))
    grad_zero = grad_cells[:fine_cells]
    zero_b = grad_zero.astype(jnp.bfloat16)
    one_b = (
        grad_cells[fine_cells:] + jnp.einsum("kr,kc->rc", up_f, grad_zero, precision=HIGH)
    ).astype(jnp.bfloat16)
    both = jnp.concatenate([zero_b, (0.25 * dot(up_b, one_b)).astype(jnp.bfloat16)], axis=1)
    both_weights = jnp.concatenate([fpn_weight[0], fpn_weight[1]], axis=1)
    grad_out = sum_to_last(dot_nt(both, both_weights), "section")

    grad_fc6 = dot_tn(grad_first, crop_rows).astype(jnp.bfloat16)
    fc6_part = lax.psum_scatter(grad_fc6, axes, scatter_dimension=0, tiled=True)
    grad_fc7 = dot_tn(grad_second, first_b).astype(jnp.bfloat16)
    fc7_part = lax.psum_scatter(grad_fc7, axes, scatter_dimension=0, tiled=True)
    fpn_terms = jnp.stack([dot_tn(top, zero_b), dot_tn(pooled, one_b)])
    grad_fpn = lax.psum(fpn_terms.astype(jnp.bfloat16), axes).astype(jnp.float32)

    kept_grad = grad_out
    for step in range(sections - 1):
        grad_in = block_backward(grad_out, normed_own, scale_own, slope_own, w_first, w_second)
        grad_out = moved(grad_in, "section", [(i + 1, i) for i in range(sections - 1)])
        kept_grad = jnp.where(section_idx == last_section - 1 - step, grad_out, kept_grad)
    all_grads = lax.all_gather(kept_grad, axes, axis=0, tiled=True)

    all_normed = norm_parts(all_tokens)[0].astype(jnp.bfloat16)
    all_slopes = gelu_parts(dot(all_normed, w_first))[1].astype(jnp.bfloat16)
    inner_part = inner_width // groups
    width_part = model_width // groups
    w_part = lax.dynamic_slice_in_dim(w_first, group_idx * inner_part, inner_part, 1)
    act_part = gelu_parts(dot(all_normed, w_part))[0].astype(jnp.bfloat16)
    normed_part = lax.dynamic_slice_in_dim(all_normed, group_idx * width_part, width_part, 1)
    all_slopes, act_part, normed_part, all_grads = lax.optimization_barrier(
        (all_slopes, act_part, normed_part, all_grads)
    )
    grad_pre = (dot_nt(all_grads, w_second) * all_slopes.astype(jnp.float32)).astype(jnp.bfloat16)
    grad_first_w = dot_tn(normed_part, grad_pre)
    grad_second_w = dot_tn(act_part, all_grads)

    fc6_out = jnp.transpose(
        fc6_part.astype(jnp.float32).reshape(-1, taps, channels), (2, 1, 0)
    )
    fc7_out = jnp.transpose(fc7_part.astype(jnp.float32))
    return (grad_first_w[None], grad_second_w[None], grad_fpn, fc6_out, fc7_out)


def solution(mesh):
    return jax.shard_map(
        per_device,
        mesh=mesh,
        in_specs=(
            P(("dp", "head"), None, None),
            P("section", None, None),
            P("section", None, None),
            P(None, None, "section"),
            P("section", None, None),
            P(),
            P(None, ("dp", "head"), None),
            P(None, None, None, ("dp", "head"), None),
            P(("dp", "head"), None, None),
            P(("dp", "head"), None, None, None),
        ),
        out_specs=(
            P("section", ("dp", "head"), None),
            P("section", ("dp", "head"), None),
            P(None, None, "section"),
            P("section", None, ("dp", "head")),
            P(None, ("dp", "head")),
        ),
        check_vma=False,
    )
```

time: 919 us -> 519 us (0.56)
  waiting for transfers between devices: 545 us -> 244 us
  local copies, waits for them, and re-layouts: 123 us -> 18.6 us
  matrix products: 118 us -> 152 us
  other arithmetic: 67 us -> 34.3 us
    reduce_scatter x3 -> x2, waiting for transfers between devices: 305 us -> 99.2 us  [the longest x1 51.3 us: per_device(): fc7_part = lax.psum_scatter(grad_fc7, axes, scatter_dimension=0, tiled=True)]
    all_gather x0 -> x2, waiting for transfers between devices: none -> 121 us  [the longest x1 60.9 us: per_device(): all_tokens = lax.all_gather(kept_tokens, axes, axis=0, tiled=True)]
    psum x4 -> x1, waiting for transfers between devices: 88.1 us -> 0.02 us  [per_device(): lax.psum(fpn_terms.astype(jnp.bfloat16), axes).astype(jnp.float32)]
    unnamed x9 -> x5, waiting for transfers between devices: 77.6 us -> 0.75 us
    all_to_all x2 -> x1, waiting for transfers between devices: 47.7 us -> 0.01 us  [box_cotangents(): lax.all_to_all(cotangent, ('dp', 'head'), split_axis=0, concat_axis=0, ti...]
    dot_general x34 -> x31, matrix products: 118 us -> 152 us  [the longest x14 82.2 us: dot(): return jnp.dot(left, right, preferred_element_type=jnp.float32)]
    scatter x1 -> x0, local copies, waits for them, and re-layouts: 28.5 us -> none  [per_device(): outgoing = jnp.zeros((groups, capacity, crop_rows.shape[1]), jnp.bfloat16...]
    unnamed x65 -> x67, local copies, waits for them, and re-layouts: 30.1 us -> 5.23 us
  transfers between devices with their start and end apart: 18 -> 19, of which waited for: 12 -> 11; matrix products, arithmetic and copies ran while one was open for 16% -> 31% of each run, Pallas kernels for 0% -> 0%
where the time goes in v1:
time: 519 us; the launch traced here: 510 us
  waiting for transfers between devices  244 us (47%)
  matrix products  152 us (29%)
  starting transfers between devices  46.6 us (9%)
  other arithmetic  34.3 us (7%)
  local copies, waits for them, and re-layouts  18.6 us (4%)
  between operations  15 us (3%)
    dot_general x14, matrix products, dot(): return jnp.dot(left, right, preferred_element_type=jnp.float32)  82.2 us
    all_gather x1, waiting for transfers between devices, per_device(): all_tokens = lax.all_gather(kept_tokens, axes, axis=0, tiled=True)  60.9 us
    all_gather x1, waiting for transfers between devices, per_device(): all_grads = lax.all_gather(kept_grad, axes, axis=0, tiled=True)  59.7 us
    dot_general x7, matrix products, dot_nt(): jnp.einsum('rk,ck->rc', left, right, preferred_element_type=jnp.float32)  57.4 us
    reduce_scatter x1, waiting for transfers between devices, per_device(): fc7_part = lax.psum_scatter(grad_fc7, axes, scatter_dimension=0, tiled=True)  51.3 us
    reduce_scatter x1, waiting for transfers between devices, per_device(): fc6_part = lax.psum_scatter(grad_fc6, axes, scatter_dimension=0, tiled=True)  47.9 us
    ppermute x13, starting transfers between devices, moved(): return lax.ppermute(block, axis, route)  39.8 us
    ppermute x13, waiting for transfers between devices, moved(): return lax.ppermute(block, axis, route)  23.3 us
  transfers between devices with their start and end apart: 19, of which 11 were waited for; matrix products, arithmetic and copies ran while one was open for 31% of the time, Pallas kernels for 0%

profile of v1, /device:TPU:0, one launch (start us, length us, event | category | flops | bytes accessed | tf_op | source)
XLA Modules:
  0.0 510.1 jit_solution(16140333917719495234)
XLA Ops:
  9.8 10.1 %fusion.87 = bf16[144,1408]{1,0:T(8,128)(2,1)} fusion(bf16[1,3072,1408]{2,1,0:T(8,128)(2,1)} %param.12, bf16[1,1408,3072]{2,1,0:T(8,128)(2,1)} %param.11, bf16[1,144,1408]{2,1,0:T(8,128)(2,1)} %param.10, f32[144]{0:T(256)S(1)} %add_rsqrt_fusion.5, f32[144]{0:T(256)S(1)} %broadcast_multiply_fusion.11), kind=kOutput, calls=%fused_computation.77 | convolution fusion | flops 2496817152 | bytes 18113664 | tf_op jit(solution)/shard_map/dot_general | solution.py:78
  22.9 6.7 %all-to-all-start = ((bf16[8,24,512]{2,1,0:T(8,128)(2,1)}), bf16[8,24,512]{2,1,0:T(8,128)(2,1)}, u32[]{:S(2)}, u32[]{:S(2)}) async-start(bf16[8,24,512]{2,1,0:T(8,128)(2,1)} %bitcast.11), calls=%async_computation | async-start | bytes 393216 | tf_op jit(solution)/shard_map/all_to_all | solution.py:137
  33.2 10.1 %fusion.84 = bf16[144,1408]{1,0:T(8,128)(2,1)} fusion(bf16[1,3072,1408]{2,1,0:T(8,128)(2,1)} %param.12, bf16[144,1408]{1,0:T(8,128)(2,1)} %collective-permute-done, bf16[1,1408,3072]{2,1,0:T(8,128)(2,1)} %param.11, f32[144]{0:T(256)S(1)} %add_rsqrt_fusion.4, f32[144]{0:T(256)S(1)} %broadcast_multiply_fusion.10), kind=kOutput, calls=%fused_computation.76 | convolution fusion | flops 2496817152 | bytes 18113664 | tf_op jit(solution)/shard_map/dot_general | solution.py:78
  48.5 10.1 %fusion.81 = bf16[144,1408]{1,0:T(8,128)(2,1)} fusion(bf16[1,3072,1408]{2,1,0:T(8,128)(2,1)} %param.12, bf16[144,1408]{1,0:T(8,128)(2,1)} %copy-done.10, bf16[1,1408,3072]{2,1,0:T(8,128)(2,1)} %param.11, f32[144]{0:T(256)S(1)} %add_rsqrt_fusion.3, f32[144]{0:T(256)S(1)} %broadcast_multiply_fusion.9), kind=kOutput, calls=%fused_computation.75 | convolution fusion | flops 2496817152 | bytes 18113664 | tf_op jit(solution)/shard_map/dot_general | solution.py:78
  58.5 6.6 %collective-permute-start.2 = (bf16[144,1408]{1,0:T(8,128)(2,1)}, bf16[144,1408]{1,0:T(8,128)(2,1)S(1)}, u32[]{:S(2)}, u32[]{:S(2)}) collective-permute-start(bf16[144,1408]{1,0:T(8,128)(2,1)} %fusion.81), channel_id=1, source_target_pairs={{0,4},{4,8},{8,12},{1,5},{5,9},{9,13},{2,6},{6,10},{10,14},{3,7},{... | collective-permute-start | bytes 1216520 | tf_op jit(solution)/shard_map/ppermute | solution.py:19
  70.1 10.0 %fusion.78 = bf16[144,1408]{1,0:T(8,128)(2,1)} fusion(bf16[1,3072,1408]{2,1,0:T(8,128)(2,1)} %param.12, bf16[144,1408]{1,0:T(8,128)(2,1)} %copy-done.11, bf16[1,1408,3072]{2,1,0:T(8,128)(2,1)} %param.11, f32[144]{0:T(256)S(1)} %add_rsqrt_fusion.2, f32[144]{0:T(256)S(1)} %broadcast_multiply_fusion.8), kind=kOutput, calls=%fused_computation.74 | convolution fusion | flops 2496817152 | bytes 18113664 | tf_op jit(solution)/shard_map/dot_general | solution.py:78
  88.4 5.7 %convert_element_type.282 = bf16[6272,180]{0,1:T(8,128)(2,1)} reshape(bf16[7,7,128,180]{2,1,0,3:T(8,128)(2,1)} %copy.41) | data formatting | bytes 4515840 | tf_op jit(solution)/shard_map/convert_element_type | solution.py:131
  94.3 3.7 collective-permute-done.4
  108.3 3.5 fusion.138
  111.8 9.2 %collective-permute-start.7 = (bf16[128,512]{1,0:T(8,128)(2,1)S(1)}, bf16[128,512]{1,0:T(8,128)(2,1)S(1)}, u32[]{:S(2)}, u32[]{:S(2)}) collective-permute-start(bf16[128,512]{1,0:T(8,128)(2,1)S(1)} %fusion.138), channel_id=1, source_target_pairs={{0,12},{4,8},{8,4},{12,0},{1,13},{5,9},{9,5},{13,1},{2,14},{6,10},... | collective-permute-start | bytes 393224 | tf_op jit(solution)/shard_map/ppermute | solution.py:19
  142.7 9.8 %collective-permute-start.9 = (bf16[144,1408]{1,0:T(8,128)(2,1)}, bf16[144,1408]{1,0:T(8,128)(2,1)}, u32[]{:S(2)}, u32[]{:S(2)}) collective-permute-start(bf16[144,1408]{1,0:T(8,128)(2,1)} %fusion.205), channel_id=1, source_target_pairs={{4,12},{5,13},{6,14},{7,15},{20,28},{21,29},{22,30},{23,31}} | collective-permute-start | bytes 1216520 | tf_op jit(solution)/shard_map/ppermute | solution.py:19
  152.5 6.1 %fusion.122 = f32[144,3072]{1,0:T(8,128)S(1)} fusion(bf16[1,1408,3072]{2,1,0:T(8,128)(2,1)} %param.11, bf16[144,1408]{1,0:T(8,128)(2,1)S(1)} %copy-done.3, f32[144]{0:T(256)S(1)} %add_rsqrt_fusion.1, f32[144]{0:T(256)S(1)} %broadcast_multiply_fusion.7), kind=kOutput, calls=%fused_computation.113 | convolution fusion | flops 1254039552 | bytes 10826880 | tf_op jit(solution)/shard_map/dot_general | solution.py:78
  163.7 12.2 %fusion.302 = (f32[144]{0:T(256)S(1)}, f32[144]{0:T(256)S(1)}, f32[144,1408]{1,0:T(8,128)}) fusion(f32[144]{0:T(256)S(1)} %add_rsqrt_fusion.1, f32[144]{0:T(256)S(1)} %broadcast_multiply_fusion.7, bf16[144,1408]{1,0:T(8,128)(2,1)S(1)} %copy-done.3, bf16[1,1408,3072]{2,1,0:T(8,128)(2,1)} %param.11, f32[144,3072]{1,0:T(8,128)S(1)} %fusion.122, ...), kind=kOutput, calls=%fused_computation.342 | convolution fusion | flops 2493517312 | bytes 20695296 | tf_op jit(solution)/shard_map/rk,ck->rc/dot_general | solution.py:82
  178.8 4.2 collective-permute-done.10
  183.0 12.0 %fusion.301 = (f32[144]{0:T(256)S(1)}, f32[144]{0:T(256)S(1)}, f32[144,1408]{1,0:T(8,128)}) fusion(f32[144]{0:T(256)S(1)} %add_rsqrt_fusion.1, f32[144]{0:T(256)S(1)} %broadcast_multiply_fusion.7, bf16[144,1408]{1,0:T(8,128)(2,1)S(1)} %copy-done.3, bf16[1,1408,3072]{2,1,0:T(8,128)(2,1)} %param.11, f32[144,3072]{1,0:T(8,128)S(1)} %fusion.122, ...), kind=kOutput, calls=%fused_computation.341 | convolution fusion | flops 2493517312 | bytes 20695296 | tf_op jit(solution)/shard_map/rk,ck->rc/dot_general | solution.py:82
  198.0 7.9 %collective-permute-done.11 = bf16[144,1408]{1,0:T(8,128)(2,1)} collective-permute-done((bf16[144,1408]{1,0:T(8,128)(2,1)S(1)}, bf16[144,1408]{1,0:T(8,128)(2,1)}, u32[]{:S(2)}, u32[]{:S(2)}) %collective-permute-start.11) | collective-permute-done | bytes 405536 | tf_op jit(solution)/shard_map/ppermute | solution.py:19
  205.9 12.1 %fusion.300 = (f32[144]{0:T(256)S(1)}, f32[144]{0:T(256)S(1)}, f32[144,1408]{1,0:T(8,128)}) fusion(f32[144]{0:T(256)S(1)} %add_rsqrt_fusion.1, f32[144]{0:T(256)S(1)} %broadcast_multiply_fusion.7, bf16[144,1408]{1,0:T(8,128)(2,1)S(1)} %copy-done.3, bf16[1,1408,3072]{2,1,0:T(8,128)(2,1)} %param.11, f32[144,3072]{1,0:T(8,128)S(1)} %fusion.122, ...), kind=kOutput, calls=%fused_computation.340 | convolution fusion | flops 2493517312 | bytes 20695296 | tf_op jit(solution)/shard_map/rk,ck->rc/dot_general | solution.py:82
  222.9 51.3 %reduce-scatter.5.cloned.1.call-done = bf16[64,512]{1,0:T(8,128)(2,1)} async-done(((bf16[512,512]{1,0:T(8,128)(2,1)}), bf16[64,512]{1,0:T(8,128)(2,1)}) %reduce-scatter.5.cloned.1.call-update) | async-done | bytes 65552 | tf_op jit(solution)/shard_map/reduce_scatter | solution.py:215
  276.6 60.9 %all-gather.3.cloned.1.call-done = bf16[1152,1408]{1,0:T(8,128)(2,1)} async-done(((bf16[144,1408]{1,0:T(8,128)(2,1)}), bf16[1152,1408]{1,0:T(8,128)(2,1)}) %all-gather.3.cloned.1.call-update) | async-done | bytes 3244048 | tf_op jit(solution)/shard_map/all_gather | solution.py:179
  343.3 4.2 fusion.112
  347.6 20.2 %fusion.5 = bf16[1152,3072]{1,0:T(8,128)(2,1)} fusion(bf16[1152,1408]{1,0:T(8,128)(2,1)S(1)} %fusion.45, bf16[1,1408,3072]{2,1,0:T(8,128)(2,1)S(1)} %bitcast.225), kind=kOutput, calls=%fused_computation.8 | convolution fusion | flops 10029367296 | bytes 18972672 | tf_op jit(solution)/shard_map/dot_general | solution.py:78
  367.8 47.9 %reduce-scatter.3.cloned.1.call-done = bf16[64,3136]{1,0:T(8,128)(2,1)} async-done(((bf16[512,3136]{1,0:T(8,128)(2,1)}), bf16[64,3136]{1,0:T(8,128)(2,1)}) %reduce-scatter.3.cloned.1.call-update) | async-done | bytes 401424 | tf_op jit(solution)/shard_map/reduce_scatter | solution.py:213
  419.3 59.7 %all-gather.5.cloned.1.call-done = bf16[1152,1408]{1,0:T(8,128)(2,1)} async-done(((bf16[144,1408]{1,0:T(8,128)(2,1)}), bf16[1152,1408]{1,0:T(8,128)(2,1)}) %all-gather.5.cloned.1.call-update) | async-done | bytes 3244048 | tf_op jit(solution)/shard_map/all_gather | solution.py:224
  479.0 18.0 %fusion.6 = bf16[1152,3072]{1,0:T(8,128)(2,1)S(1)} fusion(bf16[1152,3072]{1,0:T(8,128)(2,1)} %fusion.5, bf16[1152,1408]{1,0:T(8,128)(2,1)} %all-gather.5.cloned.1.call-done, bf16[1,3072,1408]{2,1,0:T(8,128)(2,1)} %param.12), kind=kOutput, calls=%fused_computation.9 | convolution fusion | flops 9976283136 | bytes 26050560 | tf_op jit(solution)/shard_map/rk,ck->rc/dot_general | solution.py:82
  (187 shorter events, 93.1 us)
Async XLA Ops:
  7.2 101.1 %copy-start = (bf16[64,49,512]{2,0,1:T(8,128)(2,1)S(1)}, bf16[64,49,512]{2,0,1:T(8,128)(2,1)}, u32[]{:S(2)}) copy-start(bf16[64,49,512]{2,0,1:T(8,128)(2,1)} %param.14) | copy-start | bytes 9633796
  9.7 20.0 %copy-start.23 = (f32[2,7,4,1,128]{4,3,2,1,0:T(1,128)S(1)}, f32[2,7,4,1,128]{4,3,2,1,0:T(1,128)}, u32[]{:S(2)}) copy-start(f32[2,7,4,1,128]{4,3,2,1,0:T(1,128)} %param.17) | copy-start | bytes 86020
  9.8 20.2 %copy-start.24 = (s32[3,1,128]{2,1,0:T(1,128)S(1)}, s32[3,1,128]{2,1,0:T(1,128)}, u32[]{:S(2)}) copy-start(s32[3,1,128]{2,1,0:T(1,128)} %param.16) | copy-start | bytes 4612
  19.8 11.0 %collective-permute-start = (bf16[144,1408]{1,0:T(8,128)(2,1)}, bf16[144,1408]{1,0:T(8,128)(2,1)}, u32[]{:S(2)}, u32[]{:S(2)}) collective-permute-start(bf16[144,1408]{1,0:T(8,128)(2,1)} %fusion.87), channel_id=1, source_target_pairs={{0,4},{4,8},{8,12},{1,5},{5,9},{9,13},{2,6},{6,10},{10,14},{3,7},{... | collective-permute-start | bytes 1216520 | tf_op jit(solution)/shard_map/ppermute | solution.py:19
  22.9 106.5 %all-to-all-start = ((bf16[8,24,512]{2,1,0:T(8,128)(2,1)}), bf16[8,24,512]{2,1,0:T(8,128)(2,1)}, u32[]{:S(2)}, u32[]{:S(2)}) async-start(bf16[8,24,512]{2,1,0:T(8,128)(2,1)} %bitcast.11), calls=%async_computation | async-start | bytes 393216 | tf_op jit(solution)/shard_map/all_to_all | solution.py:137
  29.6 191.4 %all-reduce.2.cloned.1.call-start = ((), (), s32[]{:S(2)}) async-start(), calls=%async_computation.5 | async-start | bytes 720896 | tf_op jit(solution)/shard_map/psum | solution.py:217
  43.3 4.2 collective-permute-start.1
  58.5 8.7 %collective-permute-start.2 = (bf16[144,1408]{1,0:T(8,128)(2,1)}, bf16[144,1408]{1,0:T(8,128)(2,1)S(1)}, u32[]{:S(2)}, u32[]{:S(2)}) collective-permute-start(bf16[144,1408]{1,0:T(8,128)(2,1)} %fusion.81), channel_id=1, source_target_pairs={{0,4},{4,8},{8,12},{1,5},{5,9},{9,13},{2,6},{6,10},{10,14},{3,7},{... | collective-permute-start | bytes 1216520 | tf_op jit(solution)/shard_map/ppermute | solution.py:19
  80.1 1.8 collective-permute-start.3
  83.7 14.3 %collective-permute-start.4 = (bf16[144,1408]{1,0:T(8,128)(2,1)}, bf16[144,1408]{1,0:T(8,128)(2,1)}, u32[]{:S(2)}, u32[]{:S(2)}) collective-permute-start(bf16[144,1408]{1,0:T(8,128)(2,1)} %broadcast_select_fusion), channel_id=1, source_target_pairs={{4,0},{12,8},{5,1},{13,9},{6,2},{14,10},{7,3},{15,11},{20,16},{28,... | collective-permute-start | bytes 1216520 | tf_op jit(solution)/shard_map/ppermute | solution.py:19
  108.3 20.2 %copy-start.16 = (bf16[512,512]{1,0:T(8,128)(2,1)S(1)}, bf16[512,512]{1,0:T(8,128)(2,1)}, u32[]{:S(2)}) copy-start(bf16[512,512]{1,0:T(8,128)(2,1)} %param.15) | copy-start | bytes 1572868
  111.8 13.1 %collective-permute-start.7 = (bf16[128,512]{1,0:T(8,128)(2,1)S(1)}, bf16[128,512]{1,0:T(8,128)(2,1)S(1)}, u32[]{:S(2)}, u32[]{:S(2)}) collective-permute-start(bf16[128,512]{1,0:T(8,128)(2,1)S(1)} %fusion.138), channel_id=1, source_target_pairs={{0,12},{4,8},{8,4},{12,0},{1,13},{5,9},{9,5},{13,1},{2,14},{6,10},... | collective-permute-start | bytes 393224 | tf_op jit(solution)/shard_map/ppermute | solution.py:19
  120.9 6.9 %collective-permute-start.6 = (bf16[128,512]{1,0:T(8,128)(2,1)S(1)}, bf16[128,512]{1,0:T(8,128)(2,1)S(1)}, u32[]{:S(2)}, u32[]{:S(2)}) collective-permute-start(bf16[128,512]{1,0:T(8,128)(2,1)S(1)} %fusion.138), channel_id=1, source_target_pairs={{0,8},{4,12},{8,0},{12,4},{1,9},{5,13},{9,1},{13,5},{2,10},{6,14},... | collective-permute-start | bytes 393224 | tf_op jit(solution)/shard_map/ppermute | solution.py:19
  122.0 5.8 %collective-permute-start.5 = (bf16[128,512]{1,0:T(8,128)(2,1)S(1)}, bf16[128,512]{1,0:T(8,128)(2,1)S(1)}, u32[]{:S(2)}, u32[]{:S(2)}) collective-permute-start(bf16[128,512]{1,0:T(8,128)(2,1)S(1)} %fusion.138), channel_id=1, source_target_pairs={{0,4},{4,0},{8,12},{12,8},{1,5},{5,1},{9,13},{13,9},{2,6},{6,2},{1... | collective-permute-start | bytes 393224 | tf_op jit(solution)/shard_map/ppermute | solution.py:19
  136.6 137.6 %reduce-scatter.5.cloned.1.call-start = ((), (), s32[]{:S(2)}) async-start(), calls=%async_computation.7 | async-start | bytes 589824 | tf_op jit(solution)/shard_map/reduce_scatter | solution.py:215
  137.8 199.7 %all-gather.3.cloned.1.call-start = ((), (), s32[]{:S(2)}) async-start(), calls=%async_computation.3 | async-start | bytes 3649536 | tf_op jit(solution)/shard_map/all_gather | solution.py:179
  138.5 277.1 %reduce-scatter.3.cloned.1.call-start = ((), (), s32[]{:S(2)}) async-start(), calls=%async_computation.6 | async-start | bytes 3686400 | tf_op jit(solution)/shard_map/reduce_scatter | solution.py:213
  139.2 2.6 collective-permute-start.8
  142.7 19.0 %collective-permute-start.9 = (bf16[144,1408]{1,0:T(8,128)(2,1)}, bf16[144,1408]{1,0:T(8,128)(2,1)}, u32[]{:S(2)}, u32[]{:S(2)}) collective-permute-start(bf16[144,1408]{1,0:T(8,128)(2,1)} %fusion.205), channel_id=1, source_target_pairs={{4,12},{5,13},{6,14},{7,15},{20,28},{21,29},{22,30},{23,31}} | collective-permute-start | bytes 1216520 | tf_op jit(solution)/shard_map/ppermute | solution.py:19
  161.6 317.4 %all-gather.5.cloned.1.call-start = ((), (), s32[]{:S(2)}) async-start(), calls=%async_computation.4 | async-start | bytes 3649536 | tf_op jit(solution)/shard_map/all_gather | solution.py:224
  177.5 5.5 %collective-permute-start.10 = (bf16[144,1408]{1,0:T(8,128)(2,1)S(1)}, bf16[144,1408]{1,0:T(8,128)(2,1)S(1)}, u32[]{:S(2)}, u32[]{:S(2)}) collective-permute-start(bf16[144,1408]{1,0:T(8,128)(2,1)S(1)} %fusion.174), channel_id=1, source_target_pairs={{4,0},{8,4},{12,8},{5,1},{9,5},{13,9},{6,2},{10,6},{14,10},{7,3},{... | collective-permute-start | bytes 1216520 | tf_op jit(solution)/shard_map/ppermute | solution.py:19
  196.5 9.4 %collective-permute-start.11 = (bf16[144,1408]{1,0:T(8,128)(2,1)S(1)}, bf16[144,1408]{1,0:T(8,128)(2,1)}, u32[]{:S(2)}, u32[]{:S(2)}) collective-permute-start(bf16[144,1408]{1,0:T(8,128)(2,1)S(1)} %fusion.179), channel_id=1, source_target_pairs={{4,0},{8,4},{12,8},{5,1},{9,5},{13,9},{6,2},{10,6},{14,10},{7,3},{... | collective-permute-start | bytes 1216520 | tf_op jit(solution)/shard_map/ppermute | solution.py:19
  219.6 56.0 %collective-permute-start.12 = (bf16[144,1408]{1,0:T(8,128)(2,1)S(1)}, bf16[144,1408]{1,0:T(8,128)(2,1)S(1)}, u32[]{:S(2)}, u32[]{:S(2)}) collective-permute-start(bf16[144,1408]{1,0:T(8,128)(2,1)S(1)} %fusion.184), channel_id=1, source_target_pairs={{4,0},{8,4},{12,8},{5,1},{9,5},{13,9},{6,2},{10,6},{14,10},{7,3},{... | collective-permute-start | bytes 1216520 | tf_op jit(solution)/shard_map/ppermute | solution.py:19
  479.0 18.0 %copy-start.26 = (bf16[1152,1408]{1,0:T(8,128)(2,1)S(1)}, bf16[1152,1408]{1,0:T(8,128)(2,1)}, u32[]{:S(2)}) copy-start(bf16[1152,1408]{1,0:T(8,128)(2,1)} %all-gather.5.cloned.1.call-done) | copy-start | bytes 9732100
  (26 other events, 130.7 us)
Sparse Core Ops, SparseCore 0:
  136.7 71.8 all-reduce.1
  212.9 61.2 reduce-scatter.4
  276.8 60.6 all-gather.2
  340.9 74.6 reduce-scatter.2
  418.4 60.6 all-gather.4

commit v2 on v1

--- a/solution.py
+++ b/solution.py
@@ -89,13 +89,13 @@
 def block_forward(tokens, w_first, w_second):
     normed, scale_inv = norm_parts(tokens)
     activ, gelu_slope = gelu_parts(dot(normed.astype(jnp.bfloat16), w_first))
-    return (tokens.astype(jnp.float32) + dot(activ.astype(jnp.bfloat16), w_second)).astype(
-        jnp.bfloat16
-    )
+    activ_b = lax.optimization_barrier(activ.astype(jnp.bfloat16))
+    return (tokens.astype(jnp.float32) + dot(activ_b, w_second)).astype(jnp.bfloat16)
 
 
 def block_backward(grad_out, normed, scale_inv, slope, w_first, w_second):
     grad_pre = (dot_nt(grad_out, w_second) * slope).astype(jnp.bfloat16)
+    grad_pre = lax.optimization_barrier(grad_pre)
     grad_norm = dot_nt(grad_pre, w_first)
     grad_tok = scale_inv * (
         grad_norm
@@ -207,21 +207,34 @@
     ).astype(jnp.bfloat16)
     both = jnp.concatenate([zero_b, (0.25 * dot(up_b, one_b)).astype(jnp.bfloat16)], axis=1)
     both_weights = jnp.concatenate([fpn_weight[0], fpn_weight[1]], axis=1)
-    grad_out = sum_to_last(dot_nt(both, both_weights), "section")
-
-    grad_fc6 = dot_tn(grad_first, crop_rows).astype(jnp.bfloat16)
-    fc6_part = lax.psum_scatter(grad_fc6, axes, scatter_dimension=0, tiled=True)
-    grad_fc7 = dot_tn(grad_second, first_b).astype(jnp.bfloat16)
-    fc7_part = lax.psum_scatter(grad_fc7, axes, scatter_dimension=0, tiled=True)
-    fpn_terms = jnp.stack([dot_tn(top, zero_b), dot_tn(pooled, one_b)])
-    grad_fpn = lax.psum(fpn_terms.astype(jnp.bfloat16), axes).astype(jnp.float32)
-
+    top_part = dot_nt(both, both_weights)
+
+    fpn_terms = jnp.concatenate([dot_tn(zero_b, top), dot_tn(one_b, pooled)], axis=0)
+    terms = jnp.concatenate(
+        [
+            dot_tn(grad_first, crop_rows).astype(jnp.bfloat16),
+            dot_tn(grad_second, first_b).astype(jnp.bfloat16),
+            fpn_terms.astype(jnp.bfloat16).reshape(head_units, -1),
+        ],
+        axis=1,
+    )
+    terms, all_tokens, top_part = lax.optimization_barrier((terms, all_tokens, top_part))
+    part = lax.psum_scatter(terms, axes, scatter_dimension=0, tiled=True)
+    fc6_part = part[:, : taps * channels]
+    fc7_part = part[:, taps * channels : taps * channels + head_units]
+    fpn_part = part[:, taps * channels + head_units :].reshape(-1, model_width)
+
+    grad_out = sum_to_last(top_part, "section")
     kept_grad = grad_out
     for step in range(sections - 1):
         grad_in = block_backward(grad_out, normed_own, scale_own, slope_own, w_first, w_second)
         grad_out = moved(grad_in, "section", [(i + 1, i) for i in range(sections - 1)])
         kept_grad = jnp.where(section_idx == last_section - 1 - step, grad_out, kept_grad)
-    all_grads = lax.all_gather(kept_grad, axes, axis=0, tiled=True)
+    token_rows = kept_grad.shape[0]
+    arrived = lax.all_gather(jnp.concatenate([kept_grad, fpn_part], axis=0), axes, axis=0)
+    all_grads = arrived[:, :token_rows].reshape(-1, model_width)
+    grad_fpn = arrived[:, token_rows:].reshape(2, channels, model_width).astype(jnp.float32)
+    grad_fpn = jnp.transpose(grad_fpn, (0, 2, 1))
 
     all_normed = norm_parts(all_tokens)[0].astype(jnp.bfloat16)
     all_slopes = gelu_parts(dot(all_normed, w_first))[1].astype(jnp.bfloat16)

time: 519 us -> 375 us (0.72)
  waiting for transfers between devices: 244 us -> 129 us
  matrix products: 152 us -> 125 us
  local copies, waits for them, and re-layouts: 18.6 us -> 30 us
  starting transfers between devices: 46.6 us -> 40.1 us
  other arithmetic: 34.3 us -> 28.3 us
    reduce_scatter x2 -> x0, waiting for transfers between devices: 99.2 us -> none  [the longest x1 51.3 us: per_device(): fc7_part = lax.psum_scatter(grad_fc7, axes, scatter_dimension=0, tiled=True)]
    unnamed x5 -> x4, waiting for transfers between devices: 0.75 us -> 35.2 us
    all_gather x1, waiting for transfers between devices: 60.9 us -> 27.5 us  [per_device(): all_tokens = lax.all_gather(kept_tokens, axes, axis=0, tiled=True)]
    all_gather x1, waiting for transfers between devices: 59.7 us -> 33 us  [per_device(): lax.all_gather(jnp.concatenate([kept_grad, fpn_part], axis=0), axes, axis=0)]
    dot_general x14 -> x18, matrix products: 82.2 us -> 67.1 us  [dot(): return jnp.dot(left, right, preferred_element_type=jnp.float32)]
    dot_general x7 -> x10, matrix products: 57.4 us -> 44.1 us  [dot_nt(): jnp.einsum('rk,ck->rc', left, right, preferred_element_type=jnp.float32)]
    ppermute x13, waiting for transfers between devices: 23.3 us -> 33.2 us  [moved(): return lax.ppermute(block, axis, route)]
    ppermute x13, starting transfers between devices: 39.8 us -> 32 us  [moved(): return lax.ppermute(block, axis, route)]
  transfers between devices with their start and end apart: 19 -> 17, of which waited for: 11 -> 13; matrix products, arithmetic and copies ran while one was open for 31% -> 40% of each run, Pallas kernels for 0% -> 0%
where the time goes in v2:
time: 375 us; the launch traced here: 367 us
  waiting for transfers between devices  129 us (34%)
  matrix products  125 us (33%)
  starting transfers between devices  40.1 us (11%)
  local copies, waits for them, and re-layouts  30 us (8%)
  other arithmetic  28.3 us (8%)
  between operations  15.4 us (4%)
    dot_general x18, matrix products, dot(): return jnp.dot(left, right, preferred_element_type=jnp.float32)  67.1 us
    dot_general x10, matrix products, dot_nt(): jnp.einsum('rk,ck->rc', left, right, preferred_element_type=jnp.float32)  44.1 us
    unnamed x4, waiting for transfers between devices  35.2 us
    ppermute x13, waiting for transfers between devices, moved(): return lax.ppermute(block, axis, route)  33.2 us
    all_gather x1, waiting for transfers between devices, per_device(): lax.all_gather(jnp.concatenate([kept_grad, fpn_part], axis=0), axes, axis=0)  33 us
    ppermute x13, starting transfers between devices, moved(): return lax.ppermute(block, axis, route)  32 us
    all_gather x1, waiting for transfers between devices, per_device(): all_tokens = lax.all_gather(kept_tokens, axes, axis=0, tiled=True)  27.5 us
    dot_general x8, matrix products, dot_tn(): jnp.einsum('kr,kc->rc', left, right, preferred_element_type=jnp.float32)  13 us
  transfers between devices with their start and end apart: 17, of which 13 were waited for; matrix products, arithmetic and copies ran while one was open for 40% of the time, Pallas kernels for 0%

profile of v2, /device:TPU:0, one launch (start us, length us, event | category | flops | bytes accessed | tf_op | source)
XLA Modules:
  0.0 367.3 jit_solution(9168840271098742749)
XLA Ops:
  7.2 7.6 %all-to-all-start = ((bf16[8,24,512]{2,1,0:T(8,128)(2,1)}), bf16[8,24,512]{2,1,0:T(8,128)(2,1)}, u32[]{:S(2)}, u32[]{:S(2)}) async-start(bf16[8,24,512]{2,1,0:T(8,128)(2,1)} %bitcast.242), calls=%async_computation | async-start | bytes 393216 | tf_op jit(solution)/shard_map/all_to_all | solution.py:137
  17.4 5.8 %fusion.95 = bf16[144,3072]{1,0:T(8,128)(2,1)S(1)} fusion(bf16[1,1408,3072]{2,1,0:T(8,128)(2,1)} %param.11, bf16[1,144,1408]{2,1,0:T(8,128)(2,1)} %param.10, f32[144]{0:T(256)S(1)} %add_rsqrt_fusion.5, f32[144]{0:T(256)S(1)} %broadcast_multiply_fusion.11), kind=kOutput, calls=%fused_computation.87 | convolution fusion | flops 1250500608 | bytes 9942144 | tf_op jit(solution)/shard_map/dot_general | solution.py:78
  31.6 5.8 %fusion.100 = bf16[144,3072]{1,0:T(8,128)(2,1)S(1)} fusion(bf16[1,1408,3072]{2,1,0:T(8,128)(2,1)} %param.11, bf16[144,1408]{1,0:T(8,128)(2,1)} %collective-permute-done, f32[144]{0:T(256)S(1)} %add_rsqrt_fusion.4, f32[144]{0:T(256)S(1)} %broadcast_multiply_fusion.10), kind=kOutput, calls=%fused_computation.92 | convolution fusion | flops 1250500608 | bytes 9942144 | tf_op jit(solution)/shard_map/dot_general | solution.py:78
  40.4 7.6 %collective-permute-start.1 = (bf16[144,1408]{1,0:T(8,128)(2,1)S(1)}, bf16[144,1408]{1,0:T(8,128)(2,1)S(1)}, u32[]{:S(2)}, u32[]{:S(2)}) collective-permute-start(bf16[144,1408]{1,0:T(8,128)(2,1)S(1)} %fusion.84), channel_id=1, source_target_pairs={{0,4},{4,8},{8,12},{1,5},{5,9},{9,13},{2,6},{6,10},{10,14},{3,7},{... | collective-permute-start | bytes 1216520 | tf_op jit(solution)/shard_map/ppermute | solution.py:19
  53.5 7.9 %collective-permute-start.2 = (bf16[144,1408]{1,0:T(8,128)(2,1)S(1)}, bf16[144,1408]{1,0:T(8,128)(2,1)S(1)}, u32[]{:S(2)}, u32[]{:S(2)}) collective-permute-start(bf16[144,1408]{1,0:T(8,128)(2,1)S(1)} %fusion.81), channel_id=1, source_target_pairs={{0,4},{4,8},{8,12},{1,5},{5,9},{9,13},{2,6},{6,10},{10,14},{3,7},{... | collective-permute-start | bytes 1216520 | tf_op jit(solution)/shard_map/ppermute | solution.py:19
  72.3 5.7 %convert_element_type.270 = bf16[6272,180]{0,1:T(8,128)(2,1)} reshape(bf16[7,7,128,180]{2,1,0,3:T(8,128)(2,1)} %copy.58) | data formatting | bytes 4515840 | tf_op jit(solution)/shard_map/convert_element_type | solution.py:131
  83.5 6.1 %collective-permute-done.4 = bf16[144,1408]{1,0:T(8,128)(2,1)} collective-permute-done((bf16[144,1408]{1,0:T(8,128)(2,1)}, bf16[144,1408]{1,0:T(8,128)(2,1)}, u32[]{:S(2)}, u32[]{:S(2)}) %collective-permute-start.4) | collective-permute-done | bytes 405536 | tf_op jit(solution)/shard_map/ppermute | solution.py:19
  94.6 3.1 convolution_convert_fusion
  100.0 3.6 fusion.136
  103.6 4.2 %collective-permute-start.7 = (bf16[128,512]{1,0:T(8,128)(2,1)S(1)}, bf16[128,512]{1,0:T(8,128)(2,1)S(1)}, u32[]{:S(2)}, u32[]{:S(2)}) collective-permute-start(bf16[128,512]{1,0:T(8,128)(2,1)S(1)} %fusion.136), channel_id=1, source_target_pairs={{0,12},{4,8},{8,4},{12,0},{1,13},{5,9},{9,5},{13,1},{2,14},{6,10},... | collective-permute-start | bytes 393224 | tf_op jit(solution)/shard_map/ppermute | solution.py:19
  127.6 27.5 %all-gather.4.cloned.1.call-done = bf16[1152,1408]{1,0:T(8,128)(2,1)} async-done(((bf16[144,1408]{1,0:T(8,128)(2,1)}), bf16[1152,1408]{1,0:T(8,128)(2,1)}) %all-gather.4.cloned.1.call-update) | async-done | bytes 3244048 | tf_op jit(solution)/shard_map/all_gather | solution.py:179
  160.3 6.1 %fusion.120 = f32[144,3072]{1,0:T(8,128)S(1)} fusion(bf16[1,1408,3072]{2,1,0:T(8,128)(2,1)} %param.11, bf16[144,1408]{1,0:T(8,128)(2,1)S(1)} %copy-done.3, f32[144]{0:T(256)S(1)} %add_rsqrt_fusion.1, f32[144]{0:T(256)S(1)} %get-tuple-element.104), kind=kOutput, calls=%fused_computation.112 | convolution fusion | flops 1254039552 | bytes 10826880 | tf_op jit(solution)/shard_map/dot_general | solution.py:78
  166.3 6.3 %copy.68 = bf16[512,4000]{1,0:T(8,128)(2,1)} copy(bf16[512,4000]{0,1:T(8,128)(2,1)} %pad_maximum_fusion) | data formatting | bytes 8192000
  174.0 6.5 %fusion.63 = bf16[144,3072]{1,0:T(8,128)(2,1)S(1)} fusion(f32[144,3072]{1,0:T(8,128)S(1)} %fusion.120, bf16[144,1408]{1,0:T(8,128)(2,1)S(1)} %add_convert_fusion, bf16[1,3072,1408]{2,1,0:T(8,128)(2,1)} %param.12), kind=kOutput, calls=%fused_computation.62 | convolution fusion | flops 1246593024 | bytes 11710464 | tf_op jit(solution)/shard_map/rk,ck->rc/dot_general | solution.py:82
  180.6 6.8 %fusion.258 = (f32[144]{0:T(256)S(1)}, f32[144]{0:T(256)S(1)}, f32[144,1408]{1,0:T(8,128)S(1)}) fusion(f32[144]{0:T(256)S(1)} %add_rsqrt_fusion.1, f32[144]{0:T(256)S(1)} %get-tuple-element.104, bf16[144,1408]{1,0:T(8,128)(2,1)S(1)} %copy-done.3, bf16[144,3072]{1,0:T(8,128)(2,1)S(1)} %fusion.63, bf16[1,1408,3072]{2,1,0:T(8,128)(2,1)} %param.11), kind=kOutput, calls=%fused_computation.328 | convolution fusion | flops 1246924544 | bytes 10754304 | tf_op jit(solution)/shard_map/rk,ck->rc/dot_general | solution.py:82
  189.3 4.7 %collective-permute-done.10 = bf16[144,1408]{1,0:T(8,128)(2,1)S(1)} collective-permute-done((bf16[144,1408]{1,0:T(8,128)(2,1)S(1)}, bf16[144,1408]{1,0:T(8,128)(2,1)S(1)}, u32[]{:S(2)}, u32[]{:S(2)}) %collective-permute-start.10) | collective-permute-done | bytes 405536 | tf_op jit(solution)/shard_map/ppermute | solution.py:19
  202.0 8.1 %collective-permute-done.11 = bf16[144,1408]{1,0:T(8,128)(2,1)S(1)} collective-permute-done((bf16[144,1408]{1,0:T(8,128)(2,1)S(1)}, bf16[144,1408]{1,0:T(8,128)(2,1)S(1)}, u32[]{:S(2)}, u32[]{:S(2)}) %collective-permute-start.11) | collective-permute-done | bytes 405536 | tf_op jit(solution)/shard_map/ppermute | solution.py:19
  220.3 5.9 %collective-permute-done.12 = bf16[144,1408]{1,0:T(8,128)(2,1)S(1)} collective-permute-done((bf16[144,1408]{1,0:T(8,128)(2,1)S(1)}, bf16[144,1408]{1,0:T(8,128)(2,1)S(1)}, u32[]{:S(2)}, u32[]{:S(2)}) %collective-permute-start.12) | collective-permute-done | bytes 405536 | tf_op jit(solution)/shard_map/ppermute | solution.py:19
  226.2 35.2 %reduce-scatter.4.cloned.1.call-done = bf16[64,4000]{1,0:T(8,128)(2,1)} async-done(((bf16[512,4000]{1,0:T(8,128)(2,1)}), bf16[64,4000]{1,0:T(8,128)(2,1)}) %reduce-scatter.4.cloned.1.call-update) | async-done | bytes 512016
  270.2 3.9 %fusion.115 = bf16[1152,384]{1,0:T(8,128)(2,1)S(1)} fusion(bf16[1152,1408]{1,0:T(8,128)(2,1)S(1)} %fusion.45, bf16[1,1408,3072]{2,1,0:T(8,128)(2,1)} %param.11, s32[]{:T(128)S(6)} %select_n.174), kind=kOutput, calls=%fused_computation.107 | convolution fusion | flops 1249689600 | bytes 5210116 | tf_op jit(solution)/shard_map/dot_general | solution.py:78
  274.2 20.1 %fusion.5 = bf16[1152,3072]{1,0:T(8,128)(2,1)} fusion(bf16[1152,1408]{1,0:T(8,128)(2,1)S(1)} %fusion.45, bf16[1,1408,3072]{2,1,0:T(8,128)(2,1)S(1)} %bitcast.231), kind=kOutput, calls=%fused_computation.8 | convolution fusion | flops 10029367296 | bytes 18972672 | tf_op jit(solution)/shard_map/dot_general | solution.py:78
  297.0 33.0 %all-gather.6.cloned.1.call-done = bf16[1280,1408]{1,0:T(8,128)(2,1)} async-done(((bf16[160,1408]{1,0:T(8,128)(2,1)}), bf16[1280,1408]{1,0:T(8,128)(2,1)}) %all-gather.6.cloned.1.call-update) | async-done | bytes 3604496 | tf_op jit(solution)/shard_map/all_gather | solution.py:234
  338.5 15.7 %fusion.6 = bf16[1152,3072]{1,0:T(8,128)(2,1)} fusion(bf16[1152,3072]{1,0:T(8,128)(2,1)} %fusion.5, bf16[1152,1408]{1,0:T(8,128)(2,1)} %bitcast.237, bf16[1,3072,1408]{2,1,0:T(8,128)(2,1)S(1)} %bitcast.225), kind=kOutput, calls=%fused_computation.9 | convolution fusion | flops 9976283136 | bytes 26050560 | tf_op jit(solution)/shard_map/rk,ck->rc/dot_general | solution.py:82
  354.2 6.1 %convolution_bitcast_fusion = f32[1,176,3072]{2,1,0:T(8,128)} fusion(bf16[1152,176]{1,0:T(8,128)(2,1)S(1)} %copy-done.11, bf16[1152,3072]{1,0:T(8,128)(2,1)} %fusion.6), kind=kOutput, calls=%fused_computation.54 | convolution fusion | flops 1245708288 | bytes 9646080 | tf_op jit(solution)/shard_map/kr,kc->rc/dot_general | solution.py:86
  (248 shorter events, 108.6 us)
Async XLA Ops:
  7.2 92.8 %copy-start = (bf16[64,49,512]{2,0,1:T(8,128)(2,1)S(1)}, bf16[64,49,512]{2,0,1:T(8,128)(2,1)}, u32[]{:S(2)}) copy-start(bf16[64,49,512]{2,0,1:T(8,128)(2,1)} %param.14) | copy-start | bytes 9633796
  7.2 108.3 %all-to-all-start = ((bf16[8,24,512]{2,1,0:T(8,128)(2,1)}), bf16[8,24,512]{2,1,0:T(8,128)(2,1)}, u32[]{:S(2)}, u32[]{:S(2)}) async-start(bf16[8,24,512]{2,1,0:T(8,128)(2,1)} %bitcast.242), calls=%async_computation | async-start | bytes 393216 | tf_op jit(solution)/shard_map/all_to_all | solution.py:137
  14.7 140.3 %all-gather.4.cloned.1.call-start = ((), (), s32[]{:S(2)}) async-start(), calls=%async_computation.2 | async-start | bytes 3649536 | tf_op jit(solution)/shard_map/all_gather | solution.py:179
  25.7 3.2 collective-permute-start
  31.5 18.1 %slice-start.12 = ((s8[8650752]{0:T(1024)(128)(4,1)}), s8[4194304]{0:T(1024)(128)(4,1)S(1)}, s32[]{:S(2)}) async-start(s8[8650752]{0:T(1024)(128)(4,1)} %bitcast.226), calls=%async_computation.17 | async-start | bytes 8388608
  40.4 8.8 %collective-permute-start.1 = (bf16[144,1408]{1,0:T(8,128)(2,1)S(1)}, bf16[144,1408]{1,0:T(8,128)(2,1)S(1)}, u32[]{:S(2)}, u32[]{:S(2)}) collective-permute-start(bf16[144,1408]{1,0:T(8,128)(2,1)S(1)} %fusion.84), channel_id=1, source_target_pairs={{0,4},{4,8},{8,12},{1,5},{5,9},{9,13},{2,6},{6,10},{10,14},{3,7},{... | collective-permute-start | bytes 1216520 | tf_op jit(solution)/shard_map/ppermute | solution.py:19
  53.5 9.2 %collective-permute-start.2 = (bf16[144,1408]{1,0:T(8,128)(2,1)S(1)}, bf16[144,1408]{1,0:T(8,128)(2,1)S(1)}, u32[]{:S(2)}, u32[]{:S(2)}) collective-permute-start(bf16[144,1408]{1,0:T(8,128)(2,1)S(1)} %fusion.81), channel_id=1, source_target_pairs={{0,4},{4,8},{8,12},{1,5},{5,9},{9,13},{2,6},{6,10},{10,14},{3,7},{... | collective-permute-start | bytes 1216520 | tf_op jit(solution)/shard_map/ppermute | solution.py:19
  68.5 9.6 %collective-permute-start.3 = (bf16[144,1408]{1,0:T(8,128)(2,1)}, bf16[144,1408]{1,0:T(8,128)(2,1)}, u32[]{:S(2)}, u32[]{:S(2)}) collective-permute-start(bf16[144,1408]{1,0:T(8,128)(2,1)} %fusion.78), channel_id=1, source_target_pairs={{12,4},{13,5},{14,6},{15,7},{28,20},{29,21},{30,22},{31,23}} | collective-permute-start | bytes 1216520 | tf_op jit(solution)/shard_map/ppermute | solution.py:19
  80.0 9.7 %collective-permute-start.4 = (bf16[144,1408]{1,0:T(8,128)(2,1)}, bf16[144,1408]{1,0:T(8,128)(2,1)}, u32[]{:S(2)}, u32[]{:S(2)}) collective-permute-start(bf16[144,1408]{1,0:T(8,128)(2,1)} %broadcast_select_fusion), channel_id=1, source_target_pairs={{4,0},{12,8},{5,1},{13,9},{6,2},{14,10},{7,3},{15,11},{20,16},{28,... | collective-permute-start | bytes 1216520 | tf_op jit(solution)/shard_map/ppermute | solution.py:19
  83.1 178.3 %reduce-scatter.4.cloned.1.call-start = ((), (), s32[]{:S(2)}) async-start(), calls=%async_computation.4 | async-start | bytes 4718592
  103.6 7.9 %collective-permute-start.7 = (bf16[128,512]{1,0:T(8,128)(2,1)S(1)}, bf16[128,512]{1,0:T(8,128)(2,1)S(1)}, u32[]{:S(2)}, u32[]{:S(2)}) collective-permute-start(bf16[128,512]{1,0:T(8,128)(2,1)S(1)} %fusion.136), channel_id=1, source_target_pairs={{0,12},{4,8},{8,4},{12,0},{1,13},{5,9},{9,5},{13,1},{2,14},{6,10},... | collective-permute-start | bytes 393224 | tf_op jit(solution)/shard_map/ppermute | solution.py:19
  107.8 6.1 %collective-permute-start.6 = (bf16[128,512]{1,0:T(8,128)(2,1)S(1)}, bf16[128,512]{1,0:T(8,128)(2,1)S(1)}, u32[]{:S(2)}, u32[]{:S(2)}) collective-permute-start(bf16[128,512]{1,0:T(8,128)(2,1)S(1)} %fusion.136), channel_id=1, source_target_pairs={{0,8},{4,12},{8,0},{12,4},{1,9},{5,13},{9,1},{13,5},{2,10},{6,14},... | collective-permute-start | bytes 393224 | tf_op jit(solution)/shard_map/ppermute | solution.py:19
  107.8 6.1 %collective-permute-start.5 = (bf16[128,512]{1,0:T(8,128)(2,1)S(1)}, bf16[128,512]{1,0:T(8,128)(2,1)S(1)}, u32[]{:S(2)}, u32[]{:S(2)}) collective-permute-start(bf16[128,512]{1,0:T(8,128)(2,1)S(1)} %fusion.136), channel_id=1, source_target_pairs={{0,4},{4,0},{8,12},{12,8},{1,5},{5,1},{9,13},{13,9},{2,6},{6,2},{1... | collective-permute-start | bytes 393224 | tf_op jit(solution)/shard_map/ppermute | solution.py:19
  125.4 31.0 %copy-start.3 = (bf16[144,1408]{1,0:T(8,128)(2,1)S(1)}, bf16[144,1408]{1,0:T(8,128)(2,1)}, u32[]{:S(2)}) copy-start(bf16[144,1408]{1,0:T(8,128)(2,1)} %get-tuple-element.61) | copy-start | bytes 1216516
  155.1 2.6 collective-permute-start.8
  158.7 14.1 %collective-permute-start.9 = (bf16[144,1408]{1,0:T(8,128)(2,1)}, bf16[144,1408]{1,0:T(8,128)(2,1)}, u32[]{:S(2)}, u32[]{:S(2)}) collective-permute-start(bf16[144,1408]{1,0:T(8,128)(2,1)} %fusion.189), channel_id=1, source_target_pairs={{4,12},{5,13},{6,14},{7,15},{20,28},{21,29},{22,30},{23,31}} | collective-permute-start | bytes 1216520 | tf_op jit(solution)/shard_map/ppermute | solution.py:19
  172.7 157.4 %all-gather.6.cloned.1.call-start = ((), (), s32[]{:S(2)}) async-start(), calls=%async_computation.3 | async-start | bytes 4055040 | tf_op jit(solution)/shard_map/all_gather | solution.py:234
  174.0 19.9 %slice-start.6 = ((s8[8650752]{0:T(1024)(128)(4,1)}), s8[4194304]{0:T(1024)(128)(4,1)S(1)}, s32[]{:S(2)}) async-start(s8[8650752]{0:T(1024)(128)(4,1)} %bitcast.222), calls=%async_computation.11 | async-start | bytes 8388608
  174.0 19.9 %slice-start.7 = ((s8[8650752]{0:T(1024)(128)(4,1)}), s8[4194304]{0:T(1024)(128)(4,1)S(1)}, s32[]{:S(2)}) async-start(s8[8650752]{0:T(1024)(128)(4,1)} %bitcast.222), calls=%async_computation.12 | async-start | bytes 8388608
  187.8 6.1 %collective-permute-start.10 = (bf16[144,1408]{1,0:T(8,128)(2,1)S(1)}, bf16[144,1408]{1,0:T(8,128)(2,1)S(1)}, u32[]{:S(2)}, u32[]{:S(2)}) collective-permute-start(bf16[144,1408]{1,0:T(8,128)(2,1)S(1)} %fusion.172), channel_id=1, source_target_pairs={{4,0},{8,4},{12,8},{5,1},{9,5},{13,9},{6,2},{10,6},{14,10},{7,3},{... | collective-permute-start | bytes 1216520 | tf_op jit(solution)/shard_map/ppermute | solution.py:19
  200.4 9.6 %collective-permute-start.11 = (bf16[144,1408]{1,0:T(8,128)(2,1)S(1)}, bf16[144,1408]{1,0:T(8,128)(2,1)S(1)}, u32[]{:S(2)}, u32[]{:S(2)}) collective-permute-start(bf16[144,1408]{1,0:T(8,128)(2,1)S(1)} %fusion.177), channel_id=1, source_target_pairs={{4,0},{8,4},{12,8},{5,1},{9,5},{13,9},{6,2},{10,6},{14,10},{7,3},{... | collective-permute-start | bytes 1216520 | tf_op jit(solution)/shard_map/ppermute | solution.py:19
  216.5 9.6 %collective-permute-start.12 = (bf16[144,1408]{1,0:T(8,128)(2,1)S(1)}, bf16[144,1408]{1,0:T(8,128)(2,1)S(1)}, u32[]{:S(2)}, u32[]{:S(2)}) collective-permute-start(bf16[144,1408]{1,0:T(8,128)(2,1)S(1)} %fusion.182), channel_id=1, source_target_pairs={{4,0},{8,4},{12,8},{5,1},{9,5},{13,9},{6,2},{10,6},{14,10},{7,3},{... | collective-permute-start | bytes 1216520 | tf_op jit(solution)/shard_map/ppermute | solution.py:19
  274.2 20.1 %copy-start.14 = (bf16[64,4000]{1,0:T(8,128)(2,1)S(1)}, bf16[64,4000]{1,0:T(8,128)(2,1)}, u32[]{:S(2)}) copy-start(bf16[64,4000]{1,0:T(8,128)(2,1)} %reduce-scatter.4.cloned.1.call-done) | copy-start | bytes 1536004
  274.2 21.1 %slice-start.21 = ((bf16[64,4000]{1,0:T(8,128)(2,1)}), bf16[64,3136]{1,0:T(8,128)(2,1)S(1)}, s32[]{:S(2)}) async-start(bf16[64,4000]{1,0:T(8,128)(2,1)} %reduce-scatter.4.cloned.1.call-done), calls=%async_computation.26 | async-start | bytes 819200 | tf_op jit(solution)/shard_map/slice | solution.py:223
  (45 other events, 301.2 us)
Sparse Core Ops, SparseCore 0:
  83.2 71.8 all-gather.3
  172.8 88.5 reduce-scatter.3
  264.3 65.7 all-gather.5

commit v3 on v2

--- a/solution.py
+++ b/solution.py
@@ -55,6 +55,11 @@
     while len(terms) > 1:
         terms = [terms[i] + terms[i + 1] for i in range(0, len(terms), 2)]
     return terms[0]
+
+
+def summed_share(blocks, axes):
+    arrived = lax.all_to_all(blocks, axes, split_axis=0, concat_axis=0, tiled=True)
+    return jnp.sum(arrived.astype(jnp.float32), axis=0)
 
 
 def gelu_parts(values):
@@ -210,19 +215,27 @@
     top_part = dot_nt(both, both_weights)
 
     fpn_terms = jnp.concatenate([dot_tn(zero_b, top), dot_tn(one_b, pooled)], axis=0)
-    terms = jnp.concatenate(
+    fpn_rows = 2 * channels // groups
+    grad_fc7 = dot_tn(grad_second, first_b).astype(jnp.bfloat16)
+    fc7_tall = grad_fc7.reshape(groups, -1, fpn_rows, head_units)
+    small = jnp.concatenate(
+        [fpn_terms.astype(jnp.bfloat16).reshape(groups, fpn_rows, model_width)]
+        + [fc7_tall[:, q] for q in range(fc7_tall.shape[1])],
+        axis=-1,
+    )
+    grad_fc6 = dot_tn(grad_first, crop_rows).astype(jnp.bfloat16)
+    grad_fc6 = grad_fc6.reshape(groups, -1, taps * channels)
+    small, grad_fc6, top_part = lax.optimization_barrier((small, grad_fc6, top_part))
+    small_part = summed_share(small, axes)
+    fc6_blocks = lax.all_to_all(grad_fc6, axes, split_axis=0, concat_axis=0, tiled=True)
+    fpn_part = small_part[:, :model_width].astype(jnp.bfloat16)
+    fc7_part = jnp.concatenate(
         [
-            dot_tn(grad_first, crop_rows).astype(jnp.bfloat16),
-            dot_tn(grad_second, first_b).astype(jnp.bfloat16),
-            fpn_terms.astype(jnp.bfloat16).reshape(head_units, -1),
+            small_part[:, model_width + q * head_units : model_width + (q + 1) * head_units]
+            for q in range(fc7_tall.shape[1])
         ],
-        axis=1,
-    )
-    terms, all_tokens, top_part = lax.optimization_barrier((terms, all_tokens, top_part))
-    part = lax.psum_scatter(terms, axes, scatter_dimension=0, tiled=True)
-    fc6_part = part[:, : taps * channels]
-    fc7_part = part[:, taps * channels : taps * channels + head_units]
-    fpn_part = part[:, taps * channels + head_units :].reshape(-1, model_width)
+        axis=0,
+    )
 
     grad_out = sum_to_last(top_part, "section")
     kept_grad = grad_out
@@ -230,6 +243,8 @@
         grad_in = block_backward(grad_out, normed_own, scale_own, slope_own, w_first, w_second)
         grad_out = moved(grad_in, "section", [(i + 1, i) for i in range(sections - 1)])
         kept_grad = jnp.where(section_idx == last_section - 1 - step, grad_out, kept_grad)
+    kept_grad, fc6_blocks = lax.optimization_barrier((kept_grad, fc6_blocks))
+    fc6_part = jnp.sum(fc6_blocks.astype(jnp.float32), axis=0)
     token_rows = kept_grad.shape[0]
     arrived = lax.all_gather(jnp.concatenate([kept_grad, fpn_part], axis=0), axes, axis=0)
     all_grads = arrived[:, :token_rows].reshape(-1, model_width)
@@ -251,9 +266,9 @@
     grad_second_w = dot_tn(act_part, all_grads)
 
     fc6_out = jnp.transpose(
-        fc6_part.astype(jnp.float32).reshape(-1, taps, channels), (2, 1, 0)
-    )
-    fc7_out = jnp.transpose(fc7_part.astype(jnp.float32))
+        fc6_part.reshape(-1, taps, channels), (2, 1, 0)
+    )
+    fc7_out = jnp.transpose(fc7_part)
     return (grad_first_w[None], grad_second_w[None], grad_fpn, fc6_out, fc7_out)
 
 

time: 375 us -> 400 us (1.067)
  matrix products: 125 us -> 140 us
  starting transfers between devices: 40.1 us -> 50.7 us
  waiting for transfers between devices: 129 us -> 133 us
    all_to_all x0 -> x2, waiting for transfers between devices: none -> 79.4 us  [the longest x1 72 us: per_device(): lax.all_to_all(grad_fc6, axes, split_axis=0, concat_axis=0, tiled=True)]
    unnamed x4 -> x2, waiting for transfers between devices: 35.2 us -> 0.03 us
    all_gather x1, waiting for transfers between devices: 27.5 us -> 0.02 us  [per_device(): all_tokens = lax.all_gather(kept_tokens, axes, axis=0, tiled=True)]
    dot_general x10, matrix products: 44.1 us -> 57.8 us  [dot_nt(): jnp.einsum('rk,ck->rc', left, right, preferred_element_type=jnp.float32)]
    all_to_all x0 -> x2, starting transfers between devices: none -> 10.4 us  [the longest x1 5.99 us: summed_share(): lax.all_to_all(blocks, axes, split_axis=0, concat_axis=0, tiled=True)]
    ppermute x13, waiting for transfers between devices: 33.2 us -> 23.4 us  [moved(): return lax.ppermute(block, axis, route)]
    unnamed x110 -> x101, local copies, waits for them, and re-layouts: 10.4 us -> 5.27 us
    convert_element_type x2 -> x1, local copies, waits for them, and re-layouts: 0.66 us -> 5.69 us  [per_device(): grad_fc6 = dot_tn(grad_first, crop_rows).astype(jnp.bfloat16)]
  transfers between devices with their start and end apart: 17 -> 18, of which waited for: 13 -> 12; matrix products, arithmetic and copies ran while one was open for 40% -> 37% of each run, Pallas kernels for 0% -> 0%
where the time goes in v3:
time: 400 us; the launch traced here: 392 us
  matrix products  140 us (35%)
  waiting for transfers between devices  133 us (33%)
  starting transfers between devices  50.7 us (13%)
  local copies, waits for them, and re-layouts  29.1 us (7%)
  other arithmetic  24.6 us (6%)
  between operations  15.6 us (4%)
    all_to_all x1, waiting for transfers between devices, per_device(): lax.all_to_all(grad_fc6, axes, split_axis=0, concat_axis=0, tiled=True)  72 us
    dot_general x18, matrix products, dot(): return jnp.dot(left, right, preferred_element_type=jnp.float32)  67.4 us
    dot_general x10, matrix products, dot_nt(): jnp.einsum('rk,ck->rc', left, right, preferred_element_type=jnp.float32)  57.8 us
    ppermute x13, starting transfers between devices, moved(): return lax.ppermute(block, axis, route)  32.4 us
    all_gather x1, waiting for transfers between devices, per_device(): lax.all_gather(jnp.concatenate([kept_grad, fpn_part], axis=0), axes, axis=0)  29.8 us
    ppermute x13, waiting for transfers between devices, moved(): return lax.ppermute(block, axis, route)  23.4 us
    dot_general x8, matrix products, dot_tn(): jnp.einsum('kr,kc->rc', left, right, preferred_element_type=jnp.float32)  13.7 us
  transfers between devices with their start and end apart: 18, of which 12 were waited for; matrix products, arithmetic and copies ran while one was open for 37% of the time, Pallas kernels for 0%

profile of v3, /device:TPU:0, one launch (start us, length us, event | category | flops | bytes accessed | tf_op | source)
XLA Modules:
  0.0 392.1 jit_solution(16470514571694039632)
XLA Ops:
  7.2 7.6 %all-to-all-start = ((bf16[8,24,512]{2,1,0:T(8,128)(2,1)}), bf16[8,24,512]{2,1,0:T(8,128)(2,1)}, u32[]{:S(2)}, u32[]{:S(2)}) async-start(bf16[8,24,512]{2,1,0:T(8,128)(2,1)} %bitcast.267), calls=%async_computation | async-start | bytes 393216 | tf_op jit(solution)/shard_map/all_to_all | solution.py:142
  17.3 5.9 %fusion.95 = bf16[144,3072]{1,0:T(8,128)(2,1)S(1)} fusion(bf16[1,1408,3072]{2,1,0:T(8,128)(2,1)} %param.11, bf16[1,144,1408]{2,1,0:T(8,128)(2,1)} %param.10, f32[144]{0:T(256)S(1)} %add_rsqrt_fusion.5, f32[144]{0:T(256)S(1)} %broadcast_multiply_fusion.11), kind=kOutput, calls=%fused_computation.87 | convolution fusion | flops 1250500608 | bytes 9942144 | tf_op jit(solution)/shard_map/dot_general | solution.py:83
  31.5 5.8 %fusion.100 = bf16[144,3072]{1,0:T(8,128)(2,1)S(1)} fusion(bf16[1,1408,3072]{2,1,0:T(8,128)(2,1)} %param.11, bf16[144,1408]{1,0:T(8,128)(2,1)} %collective-permute-done, f32[144]{0:T(256)S(1)} %add_rsqrt_fusion.4, f32[144]{0:T(256)S(1)} %broadcast_multiply_fusion.10), kind=kOutput, calls=%fused_computation.92 | convolution fusion | flops 1250500608 | bytes 9942144 | tf_op jit(solution)/shard_map/dot_general | solution.py:83
  40.4 7.7 %collective-permute-start.1 = (bf16[144,1408]{1,0:T(8,128)(2,1)S(1)}, bf16[144,1408]{1,0:T(8,128)(2,1)S(1)}, u32[]{:S(2)}, u32[]{:S(2)}) collective-permute-start(bf16[144,1408]{1,0:T(8,128)(2,1)S(1)} %fusion.84), channel_id=1, source_target_pairs={{0,4},{4,8},{8,12},{1,5},{5,9},{9,13},{2,6},{6,10},{10,14},{3,7},{... | collective-permute-start | bytes 1216520 | tf_op jit(solution)/shard_map/ppermute | solution.py:19
  53.5 7.9 %collective-permute-start.2 = (bf16[144,1408]{1,0:T(8,128)(2,1)S(1)}, bf16[144,1408]{1,0:T(8,128)(2,1)S(1)}, u32[]{:S(2)}, u32[]{:S(2)}) collective-permute-start(bf16[144,1408]{1,0:T(8,128)(2,1)S(1)} %fusion.81), channel_id=1, source_target_pairs={{0,4},{4,8},{8,12},{1,5},{5,9},{9,13},{2,6},{6,10},{10,14},{3,7},{... | collective-permute-start | bytes 1216520 | tf_op jit(solution)/shard_map/ppermute | solution.py:19
  72.3 5.7 %convert_element_type.292 = bf16[6272,180]{0,1:T(8,128)(2,1)} reshape(bf16[7,7,128,180]{2,1,0,3:T(8,128)(2,1)} %copy.84) | data formatting | bytes 4515840 | tf_op jit(solution)/shard_map/convert_element_type | solution.py:136
  82.7 5.8 %collective-permute-done.4 = bf16[144,1408]{1,0:T(8,128)(2,1)S(1)} collective-permute-done((bf16[144,1408]{1,0:T(8,128)(2,1)S(1)}, bf16[144,1408]{1,0:T(8,128)(2,1)S(1)}, u32[]{:S(2)}, u32[]{:S(2)}) %collective-permute-start.4) | collective-permute-done | bytes 405536 | tf_op jit(solution)/shard_map/ppermute | solution.py:19
  122.0 5.7 %copy.94 = bf16[512,3136]{1,0:T(8,128)(2,1)} copy(bf16[512,3136]{0,1:T(8,128)(2,1)} %convolution_convert_fusion.1) | data formatting | bytes 6422528 | tf_op jit(solution)/shard_map/convert_element_type | solution.py:226
  133.7 6.0 %fusion.120 = f32[144,3072]{1,0:T(8,128)S(1)} fusion(bf16[1,1408,3072]{2,1,0:T(8,128)(2,1)} %param.11, bf16[144,1408]{1,0:T(8,128)(2,1)S(1)} %copy-done.3, f32[144]{0:T(256)S(1)} %add_rsqrt_fusion.1, f32[144]{0:T(256)S(1)} %get-tuple-element.85), kind=kOutput, calls=%fused_computation.112 | convolution fusion | flops 1254039552 | bytes 10826880 | tf_op jit(solution)/shard_map/dot_general | solution.py:83
  139.8 6.0 %all-to-all-start.2 = ((bf16[8,16,3456]{2,1,0:T(8,128)(2,1)}), bf16[8,16,3456]{2,1,0:T(8,128)(2,1)}, u32[]{:S(2)}, u32[]{:S(2)}) async-start(bf16[8,16,3456]{2,1,0:T(8,128)(2,1)} %copy-done.16), calls=%async_computation.2 | async-start | bytes 1769472 | tf_op jit(solution)/shard_map/all_to_all | solution.py:61
  147.3 6.5 %fusion.63 = bf16[144,3072]{1,0:T(8,128)(2,1)S(1)} fusion(f32[144,3072]{1,0:T(8,128)S(1)} %fusion.120, bf16[144,1408]{1,0:T(8,128)(2,1)S(1)} %add_convert_fusion, bf16[1,3072,1408]{2,1,0:T(8,128)(2,1)} %param.12), kind=kOutput, calls=%fused_computation.62 | convolution fusion | flops 1246593024 | bytes 11710464 | tf_op jit(solution)/shard_map/rk,ck->rc/dot_general | solution.py:87
  153.8 6.6 %fusion.262 = (f32[144]{0:T(256)S(1)}, f32[144]{0:T(256)S(1)}, f32[144,1408]{1,0:T(8,128)S(1)}) fusion(f32[144]{0:T(256)S(1)} %add_rsqrt_fusion.1, f32[144]{0:T(256)S(1)} %get-tuple-element.85, bf16[144,1408]{1,0:T(8,128)(2,1)S(1)} %copy-done.3, bf16[144,3072]{1,0:T(8,128)(2,1)S(1)} %fusion.63, bf16[1,1408,3072]{2,1,0:T(8,128)(2,1)} %param.11), kind=kOutput, calls=%fused_computation.338 | convolution fusion | flops 1246924544 | bytes 10754304 | tf_op jit(solution)/shard_map/rk,ck->rc/dot_general | solution.py:87
  162.2 7.3 %all-to-all-done.2 = bf16[8,16,3456]{2,1,0:T(8,128)(2,1)} async-done(((bf16[8,16,3456]{2,1,0:T(8,128)(2,1)}), bf16[8,16,3456]{2,1,0:T(8,128)(2,1)}, u32[]{:S(2)}, u32[]{:S(2)}) %all-to-all-start.2) | async-done | bytes 884768 | tf_op jit(solution)/shard_map/all_to_all | solution.py:61
  174.0 6.6 %fusion.60 = bf16[144,3072]{1,0:T(8,128)(2,1)S(1)} fusion(f32[144,3072]{1,0:T(8,128)S(1)} %fusion.120, bf16[144,1408]{1,0:T(8,128)(2,1)S(1)} %collective-permute-done.10, bf16[1,3072,1408]{2,1,0:T(8,128)(2,1)} %param.12), kind=kOutput, calls=%fused_computation.61 | convolution fusion | flops 1246593024 | bytes 11710464 | tf_op jit(solution)/shard_map/rk,ck->rc/dot_general | solution.py:87
  180.6 6.6 %fusion.261 = (f32[144]{0:T(256)S(1)}, f32[144]{0:T(256)S(1)}, f32[144,1408]{1,0:T(8,128)S(1)}) fusion(f32[144]{0:T(256)S(1)} %add_rsqrt_fusion.1, f32[144]{0:T(256)S(1)} %get-tuple-element.85, bf16[144,1408]{1,0:T(8,128)(2,1)S(1)} %copy-done.4, bf16[144,3072]{1,0:T(8,128)(2,1)S(1)} %fusion.60, bf16[1,1408,3072]{2,1,0:T(8,128)(2,1)} %param.11), kind=kOutput, calls=%fused_computation.337 | convolution fusion | flops 1246924544 | bytes 10754304 | tf_op jit(solution)/shard_map/rk,ck->rc/dot_general | solution.py:87
  192.4 6.4 %fusion.57 = bf16[144,3072]{1,0:T(8,128)(2,1)S(1)} fusion(f32[144,3072]{1,0:T(8,128)S(1)} %fusion.120, bf16[144,1408]{1,0:T(8,128)(2,1)S(1)} %collective-permute-done.11, bf16[1,3072,1408]{2,1,0:T(8,128)(2,1)} %param.12), kind=kOutput, calls=%fused_computation.60 | convolution fusion | flops 1246593024 | bytes 11710464 | tf_op jit(solution)/shard_map/rk,ck->rc/dot_general | solution.py:87
  198.8 6.6 %fusion.260 = (f32[144]{0:T(256)S(1)}, f32[144]{0:T(256)S(1)}, f32[144,1408]{1,0:T(8,128)S(1)}) fusion(f32[144]{0:T(256)S(1)} %add_rsqrt_fusion.1, f32[144]{0:T(256)S(1)} %get-tuple-element.85, bf16[144,1408]{1,0:T(8,128)(2,1)S(1)} %copy-done.4, bf16[144,3072]{1,0:T(8,128)(2,1)S(1)} %fusion.57, bf16[1,1408,3072]{2,1,0:T(8,128)(2,1)} %param.11), kind=kOutput, calls=%fused_computation.336 | convolution fusion | flops 1246924544 | bytes 10754304 | tf_op jit(solution)/shard_map/rk,ck->rc/dot_general | solution.py:87
  209.1 6.3 %collective-permute-done.12 = bf16[144,1408]{1,0:T(8,128)(2,1)S(1)} collective-permute-done((bf16[144,1408]{1,0:T(8,128)(2,1)S(1)}, bf16[144,1408]{1,0:T(8,128)(2,1)S(1)}, u32[]{:S(2)}, u32[]{:S(2)}) %collective-permute-start.12) | collective-permute-done | bytes 405536 | tf_op jit(solution)/shard_map/ppermute | solution.py:19
  215.5 72.0 %all-to-all-done.1 = bf16[8,64,3136]{2,1,0:T(8,128)(2,1)} async-done(((bf16[8,64,3136]{2,1,0:T(8,128)(2,1)}), bf16[8,64,3136]{2,1,0:T(8,128)(2,1)}, u32[]{:S(2)}, u32[]{:S(2)}) %all-to-all-start.1) | async-done | bytes 3211296 | tf_op jit(solution)/shard_map/all_to_all | solution.py:230
  294.2 5.3 %fusion.110 = bf16[1152,384]{1,0:T(8,128)(2,1)} fusion(bf16[1152,1408]{1,0:T(8,128)(2,1)S(1)} %fusion.45, bf16[1,1408,3072]{2,1,0:T(8,128)(2,1)} %param.11, s32[]{:T(128)S(6)} %select_n.161), kind=kOutput, calls=%fused_computation.102 | convolution fusion | flops 1249689600 | bytes 5210116 | tf_op jit(solution)/shard_map/dot_general | solution.py:83
  299.5 20.1 %fusion.5 = bf16[1152,3072]{1,0:T(8,128)(2,1)} fusion(bf16[1152,1408]{1,0:T(8,128)(2,1)S(1)} %fusion.45, bf16[1,1408,3072]{2,1,0:T(8,128)(2,1)S(1)} %bitcast.250), kind=kOutput, calls=%fused_computation.8 | convolution fusion | flops 10029367296 | bytes 18972672 | tf_op jit(solution)/shard_map/dot_general | solution.py:83
  324.7 29.8 %all-gather.6.cloned.1.call-done = bf16[1280,1408]{1,0:T(8,128)(2,1)} async-done(((bf16[160,1408]{1,0:T(8,128)(2,1)}), bf16[1280,1408]{1,0:T(8,128)(2,1)}) %all-gather.6.cloned.1.call-update) | async-done | bytes 3604496 | tf_op jit(solution)/shard_map/all_gather | solution.py:249
  363.0 15.6 %fusion.6 = bf16[1152,3072]{1,0:T(8,128)(2,1)} fusion(bf16[1152,3072]{1,0:T(8,128)(2,1)} %fusion.5, bf16[1152,1408]{1,0:T(8,128)(2,1)} %bitcast.258, bf16[1,3072,1408]{2,1,0:T(8,128)(2,1)S(1)} %bitcast.246), kind=kOutput, calls=%fused_computation.9 | convolution fusion | flops 9976283136 | bytes 26050560 | tf_op jit(solution)/shard_map/rk,ck->rc/dot_general | solution.py:87
  378.7 6.1 %convolution_bitcast_fusion = f32[1,176,3072]{2,1,0:T(8,128)} fusion(bf16[1152,176]{1,0:T(8,128)(2,1)S(1)} %copy-done.13, bf16[1152,3072]{1,0:T(8,128)(2,1)} %fusion.6), kind=kOutput, calls=%fused_computation.54 | convolution fusion | flops 1245708288 | bytes 9646080 | tf_op jit(solution)/shard_map/kr,kc->rc/dot_general | solution.py:91
  (236 shorter events, 110.6 us)
Async XLA Ops:
  7.2 89.8 %copy-start = (bf16[64,49,512]{2,0,1:T(8,128)(2,1)S(1)}, bf16[64,49,512]{2,0,1:T(8,128)(2,1)}, u32[]{:S(2)}) copy-start(bf16[64,49,512]{2,0,1:T(8,128)(2,1)} %param.14) | copy-start | bytes 9633796
  7.2 105.2 %all-to-all-start = ((bf16[8,24,512]{2,1,0:T(8,128)(2,1)}), bf16[8,24,512]{2,1,0:T(8,128)(2,1)}, u32[]{:S(2)}, u32[]{:S(2)}) async-start(bf16[8,24,512]{2,1,0:T(8,128)(2,1)} %bitcast.267), calls=%async_computation | async-start | bytes 393216 | tf_op jit(solution)/shard_map/all_to_all | solution.py:142
  25.7 3.2 collective-permute-start
  31.5 18.1 %slice-start.9 = ((s8[8650752]{0:T(1024)(128)(4,1)}), s8[4194304]{0:T(1024)(128)(4,1)S(1)}, s32[]{:S(2)}) async-start(s8[8650752]{0:T(1024)(128)(4,1)} %bitcast.247), calls=%async_computation.14 | async-start | bytes 8388608
  31.5 18.1 %slice-start.10 = ((s8[8650752]{0:T(1024)(128)(4,1)}), s8[4194304]{0:T(1024)(128)(4,1)S(1)}, s32[]{:S(2)}) async-start(s8[8650752]{0:T(1024)(128)(4,1)} %bitcast.247), calls=%async_computation.15 | async-start | bytes 8388608
  40.4 8.8 %collective-permute-start.1 = (bf16[144,1408]{1,0:T(8,128)(2,1)S(1)}, bf16[144,1408]{1,0:T(8,128)(2,1)S(1)}, u32[]{:S(2)}, u32[]{:S(2)}) collective-permute-start(bf16[144,1408]{1,0:T(8,128)(2,1)S(1)} %fusion.84), channel_id=1, source_target_pairs={{0,4},{4,8},{8,12},{1,5},{5,9},{9,13},{2,6},{6,10},{10,14},{3,7},{... | collective-permute-start | bytes 1216520 | tf_op jit(solution)/shard_map/ppermute | solution.py:19
  53.5 9.2 %collective-permute-start.2 = (bf16[144,1408]{1,0:T(8,128)(2,1)S(1)}, bf16[144,1408]{1,0:T(8,128)(2,1)S(1)}, u32[]{:S(2)}, u32[]{:S(2)}) collective-permute-start(bf16[144,1408]{1,0:T(8,128)(2,1)S(1)} %fusion.81), channel_id=1, source_target_pairs={{0,4},{4,8},{8,12},{1,5},{5,9},{9,13},{2,6},{6,10},{10,14},{3,7},{... | collective-permute-start | bytes 1216520 | tf_op jit(solution)/shard_map/ppermute | solution.py:19
  68.5 9.6 %collective-permute-start.3 = (bf16[144,1408]{1,0:T(8,128)(2,1)}, bf16[144,1408]{1,0:T(8,128)(2,1)}, u32[]{:S(2)}, u32[]{:S(2)}) collective-permute-start(bf16[144,1408]{1,0:T(8,128)(2,1)} %fusion.78), channel_id=1, source_target_pairs={{12,4},{13,5},{14,6},{15,7},{28,20},{29,21},{30,22},{31,23}} | collective-permute-start | bytes 1216520 | tf_op jit(solution)/shard_map/ppermute | solution.py:19
  79.2 9.3 %collective-permute-start.4 = (bf16[144,1408]{1,0:T(8,128)(2,1)S(1)}, bf16[144,1408]{1,0:T(8,128)(2,1)S(1)}, u32[]{:S(2)}, u32[]{:S(2)}) collective-permute-start(bf16[144,1408]{1,0:T(8,128)(2,1)S(1)} %broadcast_select_fusion), channel_id=1, source_target_pairs={{4,0},{12,8},{5,1},{13,9},{6,2},{14,10},{7,3},{15,11},{20,16},{28,... | collective-permute-start | bytes 1216520 | tf_op jit(solution)/shard_map/ppermute | solution.py:19
  96.9 14.5 %copy-start.21 = (bf16[512,512]{1,0:T(8,128)(2,1)S(1)}, bf16[512,512]{1,0:T(8,128)(2,1)}, u32[]{:S(2)}) copy-start(bf16[512,512]{1,0:T(8,128)(2,1)} %param.15) | copy-start | bytes 1572868
  100.5 7.7 %collective-permute-start.7 = (bf16[128,512]{1,0:T(8,128)(2,1)S(1)}, bf16[128,512]{1,0:T(8,128)(2,1)S(1)}, u32[]{:S(2)}, u32[]{:S(2)}) collective-permute-start(bf16[128,512]{1,0:T(8,128)(2,1)S(1)} %fusion.136), channel_id=1, source_target_pairs={{0,12},{4,8},{8,4},{12,0},{1,13},{5,9},{9,5},{13,1},{2,14},{6,10},... | collective-permute-start | bytes 393224 | tf_op jit(solution)/shard_map/ppermute | solution.py:19
  104.3 6.4 %collective-permute-start.6 = (bf16[128,512]{1,0:T(8,128)(2,1)S(1)}, bf16[128,512]{1,0:T(8,128)(2,1)S(1)}, u32[]{:S(2)}, u32[]{:S(2)}) collective-permute-start(bf16[128,512]{1,0:T(8,128)(2,1)S(1)} %fusion.136), channel_id=1, source_target_pairs={{0,8},{4,12},{8,0},{12,4},{1,9},{5,13},{9,1},{13,5},{2,10},{6,14},... | collective-permute-start | bytes 393224 | tf_op jit(solution)/shard_map/ppermute | solution.py:19
  104.3 6.4 %collective-permute-start.5 = (bf16[128,512]{1,0:T(8,128)(2,1)S(1)}, bf16[128,512]{1,0:T(8,128)(2,1)S(1)}, u32[]{:S(2)}, u32[]{:S(2)}) collective-permute-start(bf16[128,512]{1,0:T(8,128)(2,1)S(1)} %fusion.136), channel_id=1, source_target_pairs={{0,4},{4,0},{8,12},{12,8},{1,5},{5,1},{9,13},{13,9},{2,6},{6,2},{1... | collective-permute-start | bytes 393224 | tf_op jit(solution)/shard_map/ppermute | solution.py:19
  128.1 3.4 collective-permute-start.8
  132.3 13.7 %collective-permute-start.9 = (bf16[144,1408]{1,0:T(8,128)(2,1)}, bf16[144,1408]{1,0:T(8,128)(2,1)}, u32[]{:S(2)}, u32[]{:S(2)}) collective-permute-start(bf16[144,1408]{1,0:T(8,128)(2,1)} %fusion.189), channel_id=1, source_target_pairs={{4,12},{5,13},{6,14},{7,15},{20,28},{21,29},{22,30},{23,31}} | collective-permute-start | bytes 1216520 | tf_op jit(solution)/shard_map/ppermute | solution.py:19
  139.8 29.7 %all-to-all-start.2 = ((bf16[8,16,3456]{2,1,0:T(8,128)(2,1)}), bf16[8,16,3456]{2,1,0:T(8,128)(2,1)}, u32[]{:S(2)}, u32[]{:S(2)}) async-start(bf16[8,16,3456]{2,1,0:T(8,128)(2,1)} %copy-done.16), calls=%async_computation.2 | async-start | bytes 1769472 | tf_op jit(solution)/shard_map/all_to_all | solution.py:61
  145.8 142.6 %all-gather.4.cloned.1.call-start = ((), (), s32[]{:S(2)}) async-start(), calls=%async_computation.3 | async-start | bytes 3649536 | tf_op jit(solution)/shard_map/all_gather | solution.py:184
  160.8 13.2 %collective-permute-start.10 = (bf16[144,1408]{1,0:T(8,128)(2,1)S(1)}, bf16[144,1408]{1,0:T(8,128)(2,1)S(1)}, u32[]{:S(2)}, u32[]{:S(2)}) collective-permute-start(bf16[144,1408]{1,0:T(8,128)(2,1)S(1)} %fusion.172), channel_id=1, source_target_pairs={{4,0},{8,4},{12,8},{5,1},{9,5},{13,9},{6,2},{10,6},{14,10},{7,3},{... | collective-permute-start | bytes 1216520 | tf_op jit(solution)/shard_map/ppermute | solution.py:19
  169.5 118.1 %all-to-all-start.1 = ((bf16[8,64,3136]{2,1,0:T(8,128)(2,1)}), bf16[8,64,3136]{2,1,0:T(8,128)(2,1)}, u32[]{:S(2)}, u32[]{:S(2)}) async-start(bf16[8,64,3136]{2,1,0:T(8,128)(2,1)} %bitcast.251), calls=%async_computation.1 | async-start | bytes 6553600 | tf_op jit(solution)/shard_map/all_to_all | solution.py:230
  174.0 180.6 %all-gather.6.cloned.1.call-start = ((), (), s32[]{:S(2)}) async-start(), calls=%async_computation.4 | async-start | bytes 4055040 | tf_op jit(solution)/shard_map/all_gather | solution.py:249
  188.3 4.0 %collective-permute-start.11 = (bf16[144,1408]{1,0:T(8,128)(2,1)}, bf16[144,1408]{1,0:T(8,128)(2,1)S(1)}, u32[]{:S(2)}, u32[]{:S(2)}) collective-permute-start(bf16[144,1408]{1,0:T(8,128)(2,1)} %fusion.177), channel_id=1, source_target_pairs={{4,0},{8,4},{12,8},{5,1},{9,5},{13,9},{6,2},{10,6},{14,10},{7,3},{... | collective-permute-start | bytes 1216520 | tf_op jit(solution)/shard_map/ppermute | solution.py:19
  205.8 9.6 %collective-permute-start.12 = (bf16[144,1408]{1,0:T(8,128)(2,1)S(1)}, bf16[144,1408]{1,0:T(8,128)(2,1)S(1)}, u32[]{:S(2)}, u32[]{:S(2)}) collective-permute-start(bf16[144,1408]{1,0:T(8,128)(2,1)S(1)} %fusion.182), channel_id=1, source_target_pairs={{4,0},{8,4},{12,8},{5,1},{9,5},{13,9},{6,2},{10,6},{14,10},{7,3},{... | collective-permute-start | bytes 1216520 | tf_op jit(solution)/shard_map/ppermute | solution.py:19
  322.6 37.4 %copy-start.30 = (bf16[1152,384]{1,0:T(8,128)(2,1)S(1)}, bf16[1152,384]{1,0:T(8,128)(2,1)}, u32[]{:S(2)}) copy-start(bf16[1152,384]{1,0:T(8,128)(2,1)} %fusion.110) | copy-start | bytes 2654212
  363.0 15.6 %copy-start.13 = (bf16[1152,176]{1,0:T(8,128)(2,1)S(1)}, bf16[1152,176]{1,0:T(8,128)(2,1)}, u32[]{:S(2)}) copy-start(bf16[1152,176]{1,0:T(8,128)(2,1)} %constant_dynamic-slice_fusion) | copy-start | bytes 1216516
  (40 other events, 229.0 us)
Sparse Core Ops, SparseCore 0:
  162.3 125.7 all-gather.3
  290.8 63.7 all-gather.5
